TPU v7x, 32 devices: a whole 2x2x4 slice. The times are simulated.
32 devices in a mesh: dp: 8 (over y, x, core), tensor: 4 (over z).
Axes of the slice: x: 2, y: 2, z: 4, core: 2. Of those that a mesh axis runs over, the one named last changes fastest.
Arguments:
- inputs: bfloat16 [16384, 768], P('dp'), may hold values from -6 to 6
- qkv_weight: bfloat16 [3, 768, 768], P(None, None, 'tensor'), may hold values from -0.21875 to 0.21875
- qv_bias: bfloat16 [2, 768], P(None, 'tensor'), may hold values from -3 to 3
- out_weight: bfloat16 [768, 768], P('tensor'), may hold values from -1.75 to 1.75
- out_bias: bfloat16 [768], replicated, may hold values from -3 to 3
- attn_gain: bfloat16 [768], replicated, may hold values from 0.25 to 1.75
- attn_shift: bfloat16 [768], replicated, may hold values from -3 to 3
- up_weight: bfloat16 [768, 3072], P(None, 'tensor'), may hold values from -0.21875 to 0.21875
- up_bias: bfloat16 [3072], P('tensor'), may hold values from -3 to 3
- down_weight: bfloat16 [3072, 768], P('tensor'), may hold values from -0.15625 to 0.15625
- down_bias: bfloat16 [768], replicated, may hold values from -3 to 3
- ffn_gain: bfloat16 [768], replicated, may hold values from 0.25 to 1.75
- ffn_shift: bfloat16 [768], replicated, may hold values from -3 to 3
- keep_mask: int32 [16], P('dp'), may hold values 0 or 1
- cotangent: bfloat16 [16384, 768], P('dp'), may hold values from -6 to 6
Outputs:
- outputs: bfloat16 [16384, 768], P('dp')
- grad_inputs: float32 [16384, 768], P('dp')
- grad_qkv: float32 [3, 768, 768], P(None, 'dp', 'tensor')
- grad_qv_bias: float32 [2, 768], P(None, 'tensor')
- grad_out_weight: float32 [768, 768], P('tensor', 'dp')
- grad_out_bias: float32 [768], replicated
- grad_attn_gain: float32 [768], replicated
- grad_attn_shift: float32 [768], replicated
- grad_up_weight: float32 [768, 3072], P('dp', 'tensor')
- grad_up_bias: float32 [3072], P('tensor')
- grad_down_weight: float32 [3072, 768], P('tensor', 'dp')
- grad_down_bias: float32 [768], replicated
- grad_ffn_gain: float32 [768], replicated
- grad_ffn_shift: float32 [768], replicated
Inputs may be any that keep to these rules, and one draw needn't show every extreme that they name: `keep_mask`: 1 keeps the layer for that sequence, 0 skips it.
All inputs are finite; a program needn't handle non-finite values. No bound on the sum of `keep_mask` on one device may be relied on, other than what follows from the above.
Results may differ from a plain program's by a relative error of at most 0.019.
The roundings to bfloat16 on the way count: a program that leaves them out, or rounds other values in their place, can miss the bound.
Values may be sent and summed in bfloat16 or wider, within the bound.
No kernel may reach another device: no remote copies, remote signals or barrier semaphores. Data moves between devices by JAX's collectives and lax.ppermute only.
A program may use at most 128 MiB of HBM per device.

v0:
```python
from functools import partial

import jax
import jax.numpy as jnp
from jax import lax
from jax.sharding import PartitionSpec as P

HEAD_DIM = 64


EPS = 1e-05


def row_norm(values):
    row_mean = jnp.mean(values, axis=-1, keepdims=True)
    centred = values - row_mean
    variance = jnp.mean(centred * centred, axis=-1, keepdims=True)
    inverse = lax.rsqrt(variance + EPS)
    return (centred * inverse, inverse)


def row_norm_back(grad_normed, normed, inverse):
    first_term = jnp.mean(grad_normed, axis=-1, keepdims=True)
    second_term = jnp.mean(grad_normed * normed, axis=-1, keepdims=True)
    return inverse * (grad_normed - first_term - normed * second_term)


def block_scores(query_block, key_vectors):
    head_dim = query_block.shape[-1]
    scores = jnp.einsum(
        "qhd,khd->hqk", query_block, key_vectors, preferred_element_type=jnp.float32
    )
    return scores * head_dim ** (-0.5)


def attend_forward(operands):
    queries, key_vectors, value_vectors = operands
    length = queries.shape[0]
    row_block = min(length, 512)
    outputs_list = []
    sums_list = []
    for offset in range(0, length, row_block):
        scores = block_scores(queries[offset : offset + row_block], key_vectors)
        row_top = jnp.max(scores, axis=-1, keepdims=True)
        exponent = jnp.exp(scores - row_top)
        row_total = jnp.sum(exponent, axis=-1, keepdims=True)
        weights = (exponent / row_total).astype(jnp.bfloat16)
        outputs_list.append(
            jnp.einsum("hqk,khd->qhd", weights, value_vectors, preferred_element_type=jnp.float32)
        )
        sums_list.append((row_top + jnp.log(row_total))[:, :, 0])
    return (jnp.concatenate(outputs_list, 0), jnp.concatenate(sums_list, 1))


def attend_backward(operands):
    queries, key_vectors, value_vectors, grad_mixed, log_sums = operands
    length = queries.shape[0]
    row_block = min(length, 512)
    score_scale = queries.shape[-1] ** (-0.5)
    grad_query_list = []
    grad_keys = jnp.zeros(key_vectors.shape, jnp.float32)
    grad_values = jnp.zeros(value_vectors.shape, jnp.float32)
    for offset in range(0, length, row_block):
        query_block = queries[offset : offset + row_block]
        grad_block = grad_mixed[offset : offset + row_block]
        scores = block_scores(query_block, key_vectors)
        weights = jnp.exp(scores - log_sums[:, offset : offset + row_block, None])
        grad_weights = jnp.einsum(
            "qhd,khd->hqk", grad_block, value_vectors, preferred_element_type=jnp.float32
        )
        row_inner = jnp.sum(weights * grad_weights, axis=-1, keepdims=True)
        grad_scores = (weights * (grad_weights - row_inner)).astype(jnp.bfloat16)
        grad_query_list.append(
            jnp.einsum("hqk,khd->qhd", grad_scores, key_vectors, preferred_element_type=jnp.float32)
            * score_scale
        )
        grad_keys = (
            grad_keys
            + jnp.einsum(
                "hqk,qhd->khd", grad_scores, query_block, preferred_element_type=jnp.float32
            )
            * score_scale
        )
        grad_values = grad_values + jnp.einsum(
            "hqk,qhd->khd",
            weights.astype(jnp.bfloat16),
            grad_block,
            preferred_element_type=jnp.float32,
        )
    grad_queries = jnp.concatenate(grad_query_list, 0)
    return (
        grad_queries.astype(jnp.bfloat16),
        grad_keys.astype(jnp.bfloat16),
        grad_values.astype(jnp.bfloat16),
    )


def per_device(
    inputs,
    qkv_weight,
    qv_bias,
    out_weight,
    out_bias,
    attn_gain,
    attn_shift,
    up_weight,
    up_bias,
    down_weight,
    down_bias,
    ffn_gain,
    ffn_shift,
    keep_mask,
    cotangent,
):
    sequences = keep_mask.shape[0]
    tokens = inputs.shape[0]
    length = tokens // sequences
    local_width = qkv_weight.shape[2]
    local_heads = local_width // HEAD_DIM
    head_shape = (sequences, length, local_heads, HEAD_DIM)
    flat_shape = (tokens, local_width)
    bias_values = qv_bias.astype(jnp.float32)
    queries = (
        jnp.dot(inputs, qkv_weight[0], preferred_element_type=jnp.float32) + bias_values[0]
    ).astype(jnp.bfloat16)
    key_vectors = jnp.dot(inputs, qkv_weight[1], preferred_element_type=jnp.float32).astype(
        jnp.bfloat16
    )
    value_vectors = (
        jnp.dot(inputs, qkv_weight[2], preferred_element_type=jnp.float32) + bias_values[1]
    ).astype(jnp.bfloat16)
    query_heads = queries.reshape(head_shape)
    key_heads = key_vectors.reshape(head_shape)
    value_heads = value_vectors.reshape(head_shape)
    mixed_heads, log_sums = lax.map(attend_forward, (query_heads, key_heads, value_heads))
    mixed_low = mixed_heads.reshape(flat_shape).astype(jnp.bfloat16)
    attention = lax.psum(
        jnp.dot(mixed_low, out_weight, preferred_element_type=jnp.float32).astype(jnp.bfloat16),
        "tensor",
    ).astype(jnp.float32) + out_bias.astype(jnp.float32)
    first_normed, first_inverse = row_norm(inputs.astype(jnp.float32) + attention)
    first_norm = first_normed * attn_gain.astype(jnp.float32) + attn_shift.astype(jnp.float32)
    first_low = first_norm.astype(jnp.bfloat16)
    pre_gelu = jnp.dot(first_low, up_weight, preferred_element_type=jnp.float32) + up_bias.astype(
        jnp.float32
    )
    active, gelu_pullback = jax.vjp(partial(jax.nn.gelu, approximate=False), pre_gelu)
    active_low = active.astype(jnp.bfloat16)
    feed = lax.psum(
        jnp.dot(active_low, down_weight, preferred_element_type=jnp.float32).astype(jnp.bfloat16),
        "tensor",
    ).astype(jnp.float32) + down_bias.astype(jnp.float32)
    second_normed, second_inverse = row_norm(first_norm + feed)
    second_norm = second_normed * ffn_gain.astype(jnp.float32) + ffn_shift.astype(jnp.float32)
    keep_rows = jnp.broadcast_to((keep_mask > 0)[:, None], (sequences, length)).reshape(tokens, 1)
    outputs = jnp.where(keep_rows, second_norm, inputs.astype(jnp.float32)).astype(jnp.bfloat16)
    grad_output = jnp.where(keep_rows, cotangent.astype(jnp.float32), 0.0)
    grad_ffn_gain = jnp.sum(grad_output * second_normed, axis=0)
    grad_ffn_shift = jnp.sum(grad_output, axis=0)
    grad_second = row_norm_back(
        grad_output * ffn_gain.astype(jnp.float32), second_normed, second_inverse
    )
    grad_down_bias = jnp.sum(grad_second, axis=0)
    grad_feed = grad_second.astype(jnp.bfloat16)
    grad_down = jnp.einsum("tf,td->fd", active_low, grad_feed, preferred_element_type=jnp.float32)
    grad_active = jnp.einsum(
        "td,fd->tf", grad_feed, down_weight, preferred_element_type=jnp.float32
    )
    grad_pre = gelu_pullback(grad_active)[0].astype(jnp.bfloat16)
    grad_up_bias = jnp.sum(grad_pre.astype(jnp.float32), axis=0)
    grad_up = jnp.einsum("td,tf->df", first_low, grad_pre, preferred_element_type=jnp.float32)
    grad_first = grad_second + lax.psum(
        jnp.einsum("tf,df->td", grad_pre, up_weight, preferred_element_type=jnp.float32).astype(
            jnp.bfloat16
        ),
        "tensor",
    ).astype(jnp.float32)
    grad_attn_gain = jnp.sum(grad_first * first_normed, axis=0)
    grad_attn_shift = jnp.sum(grad_first, axis=0)
    grad_residual = row_norm_back(
        grad_first * attn_gain.astype(jnp.float32), first_normed, first_inverse
    )
    grad_out_bias = jnp.sum(grad_residual, axis=0)
    grad_attention = grad_residual.astype(jnp.bfloat16)
    grad_out = jnp.einsum(
        "tw,td->wd", mixed_low, grad_attention, preferred_element_type=jnp.float32
    )
    grad_mixed = jnp.einsum(
        "td,wd->tw", grad_attention, out_weight, preferred_element_type=jnp.float32
    ).astype(jnp.bfloat16)
    grad_query_heads, grad_key_heads, grad_value_heads = lax.map(
        attend_backward,
        (query_heads, key_heads, value_heads, grad_mixed.reshape(head_shape), log_sums),
    )
    grad_queries = grad_query_heads.reshape(flat_shape)
    grad_keys = grad_key_heads.reshape(flat_shape)
    grad_values = grad_value_heads.reshape(flat_shape)
    grad_qkv = jnp.stack(
        [
            jnp.einsum("td,tw->dw", inputs, grad_part, preferred_element_type=jnp.float32)
            for grad_part in (grad_queries, grad_keys, grad_values)
        ]
    )
    grad_qv_bias = jnp.stack(
        [
            jnp.sum(grad_queries.astype(jnp.float32), axis=0),
            jnp.sum(grad_values.astype(jnp.float32), axis=0),
        ]
    )
    partial_input = jnp.einsum(
        "tw,dw->td", grad_queries, qkv_weight[0], preferred_element_type=jnp.float32
    )
    partial_input = partial_input + jnp.einsum(
        "tw,dw->td", grad_keys, qkv_weight[1], preferred_element_type=jnp.float32
    )
    partial_input = partial_input + jnp.einsum(
        "tw,dw->td", grad_values, qkv_weight[2], preferred_element_type=jnp.float32
    )
    summed_input = lax.psum(partial_input.astype(jnp.bfloat16), "tensor").astype(jnp.float32)
    grad_inputs = jnp.where(keep_rows, grad_residual + summed_input, cotangent.astype(jnp.float32))
    bias_grads = lax.psum(
        (
            grad_qv_bias,
            grad_out_bias,
            grad_attn_gain,
            grad_attn_shift,
            grad_up_bias,
            grad_down_bias,
            grad_ffn_gain,
            grad_ffn_shift,
        ),
        "dp",
    )
    summed = (
        lax.psum_scatter(grad_down, "dp", scatter_dimension=1, tiled=True),
        lax.psum_scatter(grad_up, "dp", scatter_dimension=0, tiled=True),
        lax.psum_scatter(grad_out, "dp", scatter_dimension=1, tiled=True),
        lax.psum_scatter(grad_qkv, "dp", scatter_dimension=1, tiled=True),
    )
    return (
        outputs,
        grad_inputs,
        summed[3],
        bias_grads[0],
        summed[2],
        bias_grads[1],
        bias_grads[2],
        bias_grads[3],
        summed[1],
        bias_grads[4],
        summed[0],
        bias_grads[5],
        bias_grads[6],
        bias_grads[7],
    )


def solution(mesh):
    placed = (
        P("dp", None),
        P(None, None, "tensor"),
        P(None, "tensor"),
        P("tensor", None),
        P(),
        P(),
        P(),
        P(None, "tensor"),
        P("tensor"),
        P("tensor", None),
        P(),
        P(),
        P(),
        P("dp"),
        P("dp", None),
    )
    return jax.shard_map(
        per_device,
        mesh=mesh,
        in_specs=placed,
        out_specs=(
            P("dp", None),
            P("dp", None),
            P(None, "dp", "tensor"),
            P(None, "tensor"),
            P("tensor", "dp"),
            P(),
            P(),
            P(),
            P("dp", "tensor"),
            P("tensor"),
            P("tensor", "dp"),
            P(),
            P(),
            P(),
        ),
        check_vma=False,
    )
```

profile of v0, /device:TPU:0, one launch (start us, length us, event | category | flops | bytes accessed | tf_op | source)
XLA Modules:
  0.0 835.7 jit_solution(16832193076168899301)
XLA Ops:
  8.1 4.1 convolution_convert_fusion.4
  15.2 3.1 fusion.103
  19.1 3.5 reshape.160
  23.9 20.3 %while.26 = (s32[]{:T(128)}, bf16[2,1024,3,64]{1,3,2,0:T(8,128)(2,1)}, f32[2,3,1024]{2,1,0:T(4,128)}, bf16[2,1024,3,64]{1,3,2,0:T(8,128)(2,1)S(1)}, bf16[2,1024,...) while((s32[]{:T(128)}, ...), condition=%wide.region_5.6_spmd, body=%wide.region_0.5_spmd.sunk | while | flops 834404352 | bytes 47524592 | solution.py:135
  47.9 3.7 convolution_convert_fusion.2
  51.8 123.8 %all-reduce.6.cloned.1.call-done = bf16[2048,768]{1,0:T(8,128)(2,1)} async-done(((bf16[2048,768]{1,0:T(8,128)(2,1)}), bf16[2048,768]{1,0:T(8,128)(2,1)}) %all-reduce.6.cloned.1.call-update) | async-done | bytes 3145744 | tf_op jit(solution)/shard_map/psum | solution.py:137
  175.5 4.1 fusion.101
  182.5 18.7 %multiply_convert_fusion.2 = (bf16[2048,768]{1,0:T(8,128)(2,1)S(1)}, f32[2048,768]{1,0:T(8,128)}, f32[2048,768]{1,0:T(8,128)}) fusion(f32[768]{0:T(1024)S(1)} %convert_element_type.156, bf16[768,768]{1,0:T(8,128)(2,1)S(1)} %copy-done, f32[768]{0:T(1024)S(1)} %convert_element_type.154, f32[768]{0:T(1024)S(1)} %convert_element_type.153, ...), kind=kOutput, calls=%fused_computation.126 | convolution fusion | flops 2533883904 | bytes 23228416 | tf_op jit(solution)/shard_map/dot_general | solution.py:144
  202.8 4.0 convolution_convert_fusion.1
  207.0 120.0 %all-reduce.8.cloned.1.call-done = bf16[2048,768]{1,0:T(8,128)(2,1)} async-done(((bf16[2048,768]{1,0:T(8,128)(2,1)}), bf16[2048,768]{1,0:T(8,128)(2,1)}) %all-reduce.8.cloned.1.call-update) | async-done | bytes 3145744 | tf_op jit(solution)/shard_map/psum | solution.py:149
  327.0 5.2 fusion.136
  334.1 4.3 fusion.93
  338.5 4.8 fusion.91
  343.4 9.5 %convert_reduce_fusion = (f32[768]{0:T(1024)}, bf16[2048,768]{1,0:T(8,128)(2,1)S(1)}) fusion(f32[2048,768]{1,0:T(8,128)S(1)} %bitcast.271, bf16[768,768]{1,0:T(8,128)(2,1)S(1)} %copy-done.68, f32[2048,768]{1,0:T(8,128)S(1)} %get-tuple-element.255, f32[2048,768]{1,0:T(8,128)} %get-tuple-element.259, f32[768]{0:T(1024)S(1)} %convert_element_type.156), kind=kOutput, calls=%fused_computation.117 | convolution fusion | flops 2444229888 | bytes 23205888 | tf_op jit(solution)/shard_map/td,fd->tf/dot_general | solution.py:166
  354.6 4.0 convolution_convert_fusion
  358.7 120.1 %all-reduce.10.cloned.1.call-done = bf16[2048,768]{1,0:T(8,128)(2,1)} async-done(((bf16[2048,768]{1,0:T(8,128)(2,1)}), bf16[2048,768]{1,0:T(8,128)(2,1)}) %all-reduce.10.cloned.1.call-update) | async-done | bytes 3145744 | tf_op jit(solution)/shard_map/psum | solution.py:172
  478.9 9.4 %multiply_reduce_fusion.4 = (f32[768]{0:T(1024)}, f32[2048]{0:T(1024)S(1)}, f32[2048]{0:T(1024)S(1)}, f32[768]{0:T(1024)}, f32[768]{0:T(1024)}) fusion(f32[2048,768]{1,0:T(8,128)} %copy-done.15, bf16[2048,768]{1,0:T(8,128)(2,1)} %all-reduce.10.cloned.1.call-done, f32[2048]{0:T(1024)S(1)} %add_rsqrt_fusion.1, f32[2048]{0:T(1024)S(1)} %broadcast_multiply_fusion.5, ...), kind=kLoop, calls=%fused_computation.118 | loop fusion | flops 25159424 | bytes 15776768 | tf_op jit(solution)/shard_map/reduce_sum | solution.py:178
  488.4 8.7 %fusion.135 = (f32[768]{0:T(1024)}, f32[2048,768]{1,0:T(8,128)}) fusion(f32[2048]{0:T(1024)S(1)} %broadcast_multiply_fusion, f32[2048]{0:T(1024)S(1)} %broadcast_multiply_fusion.5, f32[768]{0:T(1024)S(1)} %convert_element_type.152, bf16[2048,768]{1,0:T(8,128)(2,1)S(1)} %copy-done.11, bf16[2048,768]{1,0:T(8,128)(2,1)S(1)} %copy-done.5, ...), kind=kLoop, calls=%fused_computation.197 | loop fusion | flops 22019328 | bytes 22062080 | tf_op jit(solution)/shard_map/reduce_sum | solution.py:183
  497.1 5.1 fusion.113
  502.2 4.1 convolution_convert_fusion.3
  507.2 43.7 %while.27 = (s32[]{:T(128)}, bf16[2,1024,3,64]{1,3,2,0:T(8,128)(2,1)}, bf16[2,1024,3,64]{1,3,2,0:T(8,128)(2,1)}, bf16[2,1024,3,64]{1,3,2,0:T(8,128)(2,1)}, bf16[...) while((s32[]{:T(128)}, ...), condition=%wide.region_20.21_spmd, body=%wide.region_17.20_spmd.sunk | while | flops 2053174272 | bytes 131854256 | solution.py:191
  518.3 3.0 multiply_convert_fusion.4
  540.1 3.0 multiply_convert_fusion.4
  564.1 4.2 copy.61
  568.3 4.7 reshape.165
  579.8 8.2 fusion.107
  588.3 7.6 fusion.116
  598.8 24.7 %all-reduce = (f32[2,192]{1,0:T(2,128)}, f32[768]{0:T(1024)}, f32[768]{0:T(1024)}, f32[768]{0:T(1024)}, f32[768]{0:T(1024)}, /*index=5*/f32[768]{0:T(1024)}, f32[768]{0:T(1024)}, f32[768]{0:T(1024)}) all-reduce(f32[2,192]{1,0:T(2,128)S(1)} %pad_maximum_fusion.1, f32[768]{0:T(1024)S(1)} %copy-done.58, ...), channel_id=1, replica_groups=mesh['dp'=8,'tensor'=4] {'dp'}, use_global_device_ids=true, to_apply=%region_25.26 | all-reduce | flops 5760 | bytes 46080 | tf_op jit(solution)/shard_map/psum | solution.py:221
  627.1 109.0 %all-reduce.12.cloned.1.call-done = bf16[2048,768]{1,0:T(8,128)(2,1)} async-done(((bf16[2048,768]{1,0:T(8,128)(2,1)}), bf16[2048,768]{1,0:T(8,128)(2,1)}) %all-reduce.12.cloned.1.call-update) | async-done | bytes 3145744 | tf_op jit(solution)/shard_map/psum | solution.py:219
  736.1 7.6 convert_select_fusion
  743.7 38.2 %reduce-scatter.11.cloned.1.call-done = f32[768,96]{0,1:T(8,128)} async-done(((f32[768,768]{0,1:T(8,128)}), f32[768,96]{0,1:T(8,128)}) %reduce-scatter.11.cloned.1.call-update) | async-done | bytes 294928 | tf_op jit(solution)/shard_map/reduce_scatter | solution.py:235
  781.9 46.4 %reduce-scatter.9.cloned.1.call-done = f32[96,768]{1,0:T(8,128)} async-done(((f32[768,768]{1,0:T(8,128)}), f32[96,768]{1,0:T(8,128)}) %reduce-scatter.9.cloned.1.call-update) | async-done | bytes 294928 | tf_op jit(solution)/shard_map/reduce_scatter | solution.py:236
  (293 shorter events, 102.4 us)
Async XLA Ops:
  7.2 175.2 %copy-start = (bf16[768,768]{1,0:T(8,128)(2,1)S(1)}, bf16[768,768]{1,0:T(8,128)(2,1)}, u32[]{:S(2)}) copy-start(bf16[768,768]{1,0:T(8,128)(2,1)} %param.26) | copy-start | bytes 3538948
  7.2 168.3 %all-reduce.6.cloned.1.call-start = ((), (), s32[]{:S(2)}) async-start(), calls=%async_computation.4 | async-start | bytes 6291456 | tf_op jit(solution)/shard_map/psum | solution.py:137
  44.2 156.9 %copy-start.7 = (bf16[2,1024,3,64]{1,3,2,0:T(8,128)(2,1)}, bf16[2,1024,3,64]{1,3,2,0:T(8,128)(2,1)S(1)}, u32[]{:S(2)}) copy-start(bf16[2,1024,3,64]{1,3,2,0:T(8,128)(2,1)S(1)} %get-tuple-element.455) | copy-start | bytes 2359300
  51.6 275.4 %all-reduce.8.cloned.1.call-start = ((), (), s32[]{:S(2)}) async-start(), calls=%async_computation.5 | async-start | bytes 6291456 | tf_op jit(solution)/shard_map/psum | solution.py:149
  51.7 436.6 %copy-start.43 = (f32[768]{0:T(1024)}, f32[768]{0:T(1024)S(1)}, u32[]{:S(2)}) copy-start(f32[768]{0:T(1024)S(1)} %convert_element_type.152) | copy-start | bytes 9220
  51.7 436.6 %copy-start.47 = (f32[768]{0:T(1024)}, f32[768]{0:T(1024)S(1)}, u32[]{:S(2)}) copy-start(f32[768]{0:T(1024)S(1)} %convert_element_type.153) | copy-start | bytes 9220
  51.7 275.3 %copy-start.56 = (f32[768]{0:T(1024)}, f32[768]{0:T(1024)S(1)}, u32[]{:S(2)}) copy-start(f32[768]{0:T(1024)S(1)} %convert_element_type.154) | copy-start | bytes 9220
  180.2 308.1 %copy-start.38 = (f32[2048]{0:T(1024)}, f32[2048]{0:T(1024)S(1)}, u32[]{:S(2)}) copy-start(f32[2048]{0:T(1024)S(1)} %broadcast_multiply_fusion.5) | copy-start | bytes 24580
  182.4 305.9 %copy-start.45 = (f32[2048]{0:T(1024)}, f32[2048]{0:T(1024)S(1)}, u32[]{:S(2)}) copy-start(f32[2048]{0:T(1024)S(1)} %add_rsqrt_fusion.1) | copy-start | bytes 24580
  182.4 20.3 %copy-start.67 = (bf16[768,768]{1,0:T(8,128)(2,1)S(1)}, bf16[768,768]{1,0:T(8,128)(2,1)}, u32[]{:S(2)}) copy-start(bf16[768,768]{1,0:T(8,128)(2,1)} %param.28) | copy-start | bytes 3538948
  206.8 272.1 %all-reduce.10.cloned.1.call-start = ((), (), s32[]{:S(2)}) async-start(), calls=%async_computation.6 | async-start | bytes 6291456 | tf_op jit(solution)/shard_map/psum | solution.py:172
  207.0 131.5 %copy-start.49 = (pred[2048]{0:T(1024)(128)(4,1)}, pred[2048]{0:T(1024)(128)(4,1)S(1)}, u32[]{:S(2)}) copy-start(pred[2048]{0:T(1024)(128)(4,1)S(1)} %broadcast_in_dim.47) | copy-start | bytes 6148
  334.1 9.2 %slice-start = ((s8[6291456]{0:T(1024)(128)(4,1)}), s8[4194304]{0:T(1024)(128)(4,1)S(1)}, s32[]{:S(2)}) async-start(s8[6291456]{0:T(1024)(128)(4,1)} %bitcast.270), calls=%async_computation.12 | async-start | bytes 8388608
  343.4 9.5 %copy-start.15 = (f32[2048,768]{1,0:T(8,128)}, f32[2048,768]{1,0:T(8,128)S(1)}, u32[]{:S(2)}) copy-start(f32[2048,768]{1,0:T(8,128)S(1)} %get-tuple-element.255) | copy-start | bytes 18874372
  358.7 264.9 %reduce-scatter.15.cloned.1.call-start = ((), (), s32[]{:S(2)}) async-start(), calls=%async_computation.11 | async-start | bytes 884736
  358.7 129.6 %copy-start.5 = (bf16[2048,768]{1,0:T(8,128)(2,1)S(1)}, bf16[2048,768]{1,0:T(8,128)(2,1)}, u32[]{:S(2)}) copy-start(bf16[2048,768]{1,0:T(8,128)(2,1)} %param.19) | copy-start | bytes 9437188
  478.9 9.5 %copy-start.11 = (bf16[2048,768]{1,0:T(8,128)(2,1)S(1)}, bf16[2048,768]{1,0:T(8,128)(2,1)}, u32[]{:S(2)}) copy-start(bf16[2048,768]{1,0:T(8,128)(2,1)} %all-reduce.6.cloned.1.call-done) | copy-start | bytes 9437188
  478.9 9.5 %copy-start.21 = (bf16[2048,768]{1,0:T(8,128)(2,1)S(1)}, bf16[2048,768]{1,0:T(8,128)(2,1)}, u32[]{:S(2)}) copy-start(bf16[2048,768]{1,0:T(8,128)(2,1)} %all-reduce.10.cloned.1.call-done) | copy-start | bytes 9437188
  506.3 118.9 %reduce-scatter.13.cloned.1.call-start = ((), (), s32[]{:S(2)}) async-start(), calls=%async_computation.10 | async-start | bytes 2211840
  573.1 163.0 %all-reduce.12.cloned.1.call-start = ((), (), s32[]{:S(2)}) async-start(), calls=%async_computation.7 | async-start | bytes 6291456 | tf_op jit(solution)/shard_map/psum | solution.py:219
  579.5 8.8 %copy-start.39 = (f32[2048]{0:T(1024)S(1)}, f32[2048]{0:T(1024)}, u32[]{:S(2)}) copy-start(f32[2048]{0:T(1024)} %copy-done.38) | copy-start | bytes 24580
  579.5 202.4 %reduce-scatter.11.cloned.1.call-start = ((), (), s32[]{:S(2)}) async-start(), calls=%async_computation.9 | async-start | bytes 2654208 | tf_op jit(solution)/shard_map/reduce_scatter | solution.py:235
  588.1 10.7 %copy-start.51 = (f32[768]{0:T(1024)S(1)}, f32[768]{0:T(1024)}, u32[]{:S(2)}) copy-start(f32[768]{0:T(1024)} %get-tuple-element.190) | copy-start | bytes 9220
  588.1 10.7 %copy-start.52 = (f32[768]{0:T(1024)S(1)}, f32[768]{0:T(1024)}, u32[]{:S(2)}) copy-start(f32[768]{0:T(1024)} %get-tuple-element.196) | copy-start | bytes 9220
  588.1 10.7 %copy-start.53 = (f32[768]{0:T(1024)S(1)}, f32[768]{0:T(1024)}, u32[]{:S(2)}) copy-start(f32[768]{0:T(1024)} %get-tuple-element.188) | copy-start | bytes 9220
  588.1 10.7 %copy-start.54 = (f32[768]{0:T(1024)S(1)}, f32[768]{0:T(1024)}, u32[]{:S(2)}) copy-start(f32[768]{0:T(1024)} %get-tuple-element.193) | copy-start | bytes 9220
  588.2 10.7 %copy-start.55 = (f32[768]{0:T(1024)S(1)}, f32[768]{0:T(1024)}, u32[]{:S(2)}) copy-start(f32[768]{0:T(1024)} %get-tuple-element.194) | copy-start | bytes 9220
  588.2 10.7 %copy-start.58 = (f32[768]{0:T(1024)S(1)}, f32[768]{0:T(1024)}, u32[]{:S(2)}) copy-start(f32[768]{0:T(1024)} %get-tuple-element.235) | copy-start | bytes 9220
  588.2 10.7 %copy-start.59 = (f32[768]{0:T(1024)S(1)}, f32[768]{0:T(1024)}, u32[]{:S(2)}) copy-start(f32[768]{0:T(1024)} %get-tuple-element.260) | copy-start | bytes 9220
  588.2 147.9 %copy-start.50 = (pred[2048]{0:T(1024)(128)(4,1)S(1)}, pred[2048]{0:T(1024)(128)(4,1)}, u32[]{:S(2)}) copy-start(pred[2048]{0:T(1024)(128)(4,1)} %copy-done.49) | copy-start | bytes 6148
  588.2 240.2 %reduce-scatter.9.cloned.1.call-start = ((), (), s32[]{:S(2)}) async-start(), calls=%async_computation.8 | async-start | bytes 2654208 | tf_op jit(solution)/shard_map/reduce_scatter | solution.py:236
  626.3 202.1 %copy-start.1 = (bf16[768,768]{1,0:T(8,128)(2,1)S(1)}, bf16[768,768]{1,0:T(8,128)(2,1)}, u32[]{:S(2)}) copy-start(bf16[768,768]{1,0:T(8,128)(2,1)} %param.26) | copy-start | bytes 3538948
  (63 other events, 245.7 us)
Sparse Core Ops, SparseCore 0:
  51.7 123.7 all-reduce.5
  206.9 120.0 all-reduce.7
  358.8 120.0 all-reduce.9
  506.4 33.9 reduce-scatter.14
  573.2 39.3 reduce-scatter.12
  614.9 121.1 all-reduce.11
  740.4 41.5 reduce-scatter.10
  785.9 42.4 reduce-scatter.8
where the time goes:
time: 840 us; the launch traced here: 836 us
  waiting for transfers between devices  558 us (66%)
  matrix products  130 us (15%)
  other arithmetic  62.9 us (7%)
  local copies, waits for them, and re-layouts  43.4 us (5%)
  blocking collectives  24.7 us (3%)
  between operations  15.5 us (2%)
    psum x1, waiting for transfers between devices, per_device(): lax.psum(jnp.dot(mixed_low, out_weight, preferred_element_type=jnp.float3...  124 us
    psum x1, waiting for transfers between devices, per_device(): lax.psum(jnp.einsum('tf,df->td', grad_pre, up_weight, preferred_element_t...  120 us
    psum x1, waiting for transfers between devices, per_device(): lax.psum(jnp.dot(active_low, down_weight, preferred_element_type=jnp.floa...  120 us
    psum x1, waiting for transfers between devices, per_device(): lax.psum(partial_input.astype(jnp.bfloat16), 'tensor').astype(jnp.float32)  109 us
    reduce_scatter x1, waiting for transfers between devices, per_device(): lax.psum_scatter(grad_up, 'dp', scatter_dimension=0, tiled=True)  46.4 us
    reduce_scatter x1, waiting for transfers between devices, per_device(): lax.psum_scatter(grad_down, 'dp', scatter_dimension=1, tiled=True)  38.2 us
    psum x1, blocking collectives, per_device(): lax.psum((grad_qv_bias, grad_out_bias, grad_attn_gain, grad_attn_shift, g...  24.7 us
    unnamed x131, local copies, waits for them, and re-layouts  21.2 us
  transfers between devices with their start and end apart: 8, of which 6 were waited for; matrix products, arithmetic and copies ran while one was open for 12% of the time, Pallas kernels for 0%

commit v1 on v0

v1 whole, which is shorter than its diff:
```python
from functools import partial

import jax
import jax.numpy as jnp
import numpy as np
from jax import lax
from jax.experimental import pallas as pl
from jax.experimental.pallas import tpu as pltpu
from jax.sharding import PartitionSpec as P

HEAD_DIM = 64
EPS = 1e-05
LOG2E = 1.4426950408889634
BF = jnp.bfloat16
F32 = jnp.float32
ANY = pl.BlockSpec(memory_space=pl.ANY)
VM = pl.BlockSpec(memory_space=pltpu.VMEM)
LIMIT = 60 * 1024 * 1024


def nn(a, b):
    return lax.dot_general(a, b, (((1,), (0,)), ((), ())), preferred_element_type=F32)


def nt(a, b):
    return lax.dot_general(a, b, (((1,), (1,)), ((), ())), preferred_element_type=F32)


def cost(us):
    return pl.CostEstimate(flops=int(us * 9e8), bytes_accessed=1024, transcendentals=0)


def params(**kw):
    return pltpu.CompilerParams(vmem_limit_bytes=LIMIT, **kw)


def head_mask(rows, width, head):
    lane = lax.broadcasted_iota(jnp.int32, (rows, width), 1)
    return (lane >= head * HEAD_DIM) & (lane < (head + 1) * HEAD_DIM)


def row_norm(values):
    row_mean = jnp.mean(values, axis=-1, keepdims=True)
    centred = values - row_mean
    variance = jnp.mean(centred * centred, axis=-1, keepdims=True)
    inverse = lax.rsqrt(variance + EPS)
    return centred * inverse, inverse


def row_norm_back(grad_normed, normed, inverse):
    first_term = jnp.mean(grad_normed, axis=-1, keepdims=True)
    second_term = jnp.mean(grad_normed * normed, axis=-1, keepdims=True)
    return inverse * (grad_normed - first_term - normed * second_term)


def gelu_both(x):
    e = jnp.exp2(x * x * (-0.5 * LOG2E))
    t = 1.0 / (1.0 + (0.3275911 * 0.7071067811865476) * jnp.abs(x))
    poly = t * (
        0.5 * 0.254829592
        + t
        * (
            0.5 * -0.284496736
            + t * (0.5 * 1.421413741 + t * (0.5 * -1.453152027 + t * (0.5 * 1.061405429)))
        )
    )
    tail = poly * e
    cdf = jnp.where(x < 0, tail, 1.0 - tail)
    return x * cdf, cdf + x * (e * 0.3989422804014327)


def place_copies(pieces, parts, meta, sems):
    copies = []
    index = 0
    for place, piece in enumerate(pieces):
        quarter = meta[1] ^ (place % 4)
        side = meta[2] ^ (place // 4)
        lanes = piece.shape[2]
        for scratch, first, rows, spread in parts:
            start = pl.multiple_of(quarter * rows + spread, 16)
            copies.append(
                pltpu.make_async_copy(
                    piece.at[:, pl.ds(first, rows), :],
                    scratch.at[:, pl.ds(start, rows), pl.ds(pl.multiple_of(side * lanes, 128), lanes)],
                    sems.at[index],
                )
            )
            index += 1
    return copies


def attend_kernel(meta, x_ref, w_ref, b_ref, o0_ref, o1_ref, l0_ref, l1_ref, q_s, k_s, v_s):
    x = x_ref[...]
    length, width = q_s.shape
    heads = width // HEAD_DIM
    half = length // 2
    scale = HEAD_DIM ** (-0.5) * LOG2E
    q_s[...] = (nn(x, w_ref[0]) + b_ref[0:1, :].astype(F32)).astype(BF)
    k_s[...] = nn(x, w_ref[1]).astype(BF)
    v_s[...] = (nn(x, w_ref[2]) + b_ref[1:2, :].astype(F32)).astype(BF)
    block = 256
    for k, (o_ref, l_ref) in enumerate(((o0_ref, l0_ref), (o1_ref, l1_ref))):
        start = ((meta[0] % 2) ^ k) * half
        for part in range(half // block):
            rows = pl.ds(pl.multiple_of(start + part * block, block), block)
            q = q_s[rows, :]
            mixed = jnp.zeros((block, width), F32)
            stats = jnp.zeros((block, 128), F32)
            stat_lane = lax.broadcasted_iota(jnp.int32, (block, 128), 1)
            for h in range(heads):
                mask = head_mask(block, width, h)
                s = nt(jnp.where(mask, q, jnp.zeros_like(q)), k_s[...])
                top = jnp.max(s, axis=-1, keepdims=True)
                p = jnp.exp2((s - top) * scale)
                total = jnp.sum(p, axis=-1, keepdims=True)
                o = nn(p.astype(BF), v_s[...]) * (1.0 / total)
                mixed = jnp.where(mask, o, mixed)
                stats = jnp.where(stat_lane == h, top * scale + jnp.log2(total), stats)
            o_ref[part * block : (part + 1) * block, :] = mixed.astype(BF)
            l_ref[:, part * block : (part + 1) * block] = jnp.transpose(stats)[:8, :]


def attend(meta, inputs, qkv_weight, qv_bias, length, other):
    width = qkv_weight.shape[2]
    dim = inputs.shape[1]
    half = length // 2
    return pl.pallas_call(
        attend_kernel,
        grid_spec=pltpu.PrefetchScalarGridSpec(
            num_scalar_prefetch=1,
            grid=(1,),
            in_specs=[
                pl.BlockSpec((length, dim), lambda i, m: ((m[0] // 2) ^ other, 0)),
                VM,
                VM,
            ],
            out_specs=[VM] * 4,
            scratch_shapes=[pltpu.VMEM((length, width), BF)] * 3,
        ),
        out_shape=[jax.ShapeDtypeStruct((half, width), BF)] * 2
        + [jax.ShapeDtypeStruct((8, half), F32)] * 2,
        compiler_params=params(),
        cost_estimate=cost(8),
    )(meta, inputs, qkv_weight, qv_bias)


def up_kernel(
    meta, x_ref, o0, o1, o2, o3, ob_ref, ag_ref, as_ref, ub_ref, wo_ref, wu_ref,
    p0, p1, p2, p3, p4, p5, p6, p7,
    n1_ref, r1_ref, ulow_ref, act_ref, der_ref, wo_s, wu_s, sems,
):
    dim = x_ref.shape[1]
    up_rows = wu_ref.shape[0] // 4
    out_rows = wo_ref.shape[0] // 4
    pieces = (p0, p1, p2, p3, p4, p5, p6, p7)
    out_copies = place_copies(pieces, ((wo_s, up_rows, out_rows, 0),), meta, sems.at[0])
    up_copies = place_copies(pieces, ((wu_s, 0, up_rows, 0),), meta, sems.at[1])
    for copy in out_copies + up_copies:
        copy.start()
    total = x_ref[...].astype(F32) + ob_ref[...].astype(F32) + nn(o0[...], wo_ref[...])
    for copy in out_copies:
        copy.wait()
    for r, o_ref in ((1, o1), (2, o2), (3, o3)):
        total = total + nn(o_ref[...], wo_s[r - 1])
    normed, inverse = row_norm(total)
    n1_ref[...] = normed
    r1_ref[...] = inverse
    low = (normed * ag_ref[...].astype(F32) + as_ref[...].astype(F32)).astype(BF)
    ulow_ref[...] = low

    def hidden(r, weight):
        for c in range(0, dim, 256):
            z = nn(ulow_ref[...], weight[:, c : c + 256]) + ub_ref[r : r + 1, c : c + 256].astype(F32)
            act, der = gelu_both(z)
            act_ref[r, :, c : c + 256] = act.astype(BF)
            der_ref[r, :, c : c + 256] = der.astype(BF)

    hidden(0, wu_ref)
    for copy in up_copies:
        copy.wait()
    for r in range(1, 4):
        hidden(r, wu_s.at[r - 1])


def down_kernel(
    meta, n1_ref, ag_ref, as_ref, db_ref, fg_ref, fs_ref, act_ref, x_ref, cot_ref, wd_ref,
    p0, p1, p2, p3, p4, p5, p6, p7,
    out_ref, dh2_ref, df_ref, small_ref, wd_s, sems,
):
    pieces = (p0, p1, p2, p3, p4, p5, p6, p7)
    copies = place_copies(pieces, ((wd_s, 0, wd_ref.shape[0] // 4, 0),), meta, sems)
    for copy in copies:
        copy.start()
    first = n1_ref[...] * ag_ref[...].astype(F32) + as_ref[...].astype(F32)
    total = first + db_ref[...].astype(F32) + nn(act_ref[0], wd_ref[...])
    for copy in copies:
        copy.wait()
    for r in range(1, 4):
        total = total + nn(act_ref[r], wd_s[r - 1])
    normed, inverse = row_norm(total)
    gain = fg_ref[...].astype(F32)
    keep = meta[3] > 0
    second = normed * gain + fs_ref[...].astype(F32)
    out_ref[...] = jnp.where(keep, second, x_ref[...].astype(F32)).astype(BF)
    grad = jnp.where(keep, cot_ref[...].astype(F32), 0.0)
    dh2 = row_norm_back(grad * gain, normed, inverse)
    dh2_ref[...] = dh2
    df_ref[...] = dh2.astype(BF)
    small_ref[...] = jnp.zeros_like(small_ref)
    small_ref[0:1, :] = jnp.sum(grad * normed, axis=0, keepdims=True)
    small_ref[1:2, :] = jnp.sum(grad, axis=0, keepdims=True)
    small_ref[2:3, :] = jnp.sum(dh2, axis=0, keepdims=True)


def ffn_back_kernel(
    meta, df_ref, dh2_ref, der_ref, n1_ref, r1_ref, ag_ref, o0, o1, o2, o3, wd_ref, wu_ref, wo_ref,
    d0, d1, d2, d3, d4, d5, d6, d7, p0, p1, p2, p3, p4, p5, p6, p7,
    dz_ref, dh1_ref, da_ref, do_ref, delta_ref, small_ref, wd_s, wu_s, wo_s, sems,
):
    dim = df_ref.shape[1]
    up_rows = wu_ref.shape[0] // 4
    out_rows = wo_ref.shape[0] // 4
    downs = (d0, d1, d2, d3, d4, d5, d6, d7)
    pieces = (p0, p1, p2, p3, p4, p5, p6, p7)
    down_copies = place_copies(downs, ((wd_s, 0, wd_ref.shape[0] // 4, 0),), meta, sems.at[0])
    up_copies = place_copies(pieces, ((wu_s, 0, up_rows, 0),), meta, sems.at[1])
    out_copies = place_copies(pieces, ((wo_s, up_rows, out_rows, 0),), meta, sems.at[2])
    for copy in down_copies + up_copies + out_copies:
        copy.start()
    small_ref[...] = jnp.zeros_like(small_ref)
    dh1_ref[...] = dh2_ref[...]

    def hidden(r, down, up):
        for c in range(0, dim, 256):
            dz = (nt(df_ref[...], down[c : c + 256, :]) * der_ref[r, :, c : c + 256].astype(F32)).astype(BF)
            dz_ref[r, :, c : c + 256] = dz
            small_ref[8 + r : 9 + r, c : c + 256] = jnp.sum(dz.astype(F32), axis=0, keepdims=True)
        dh1_ref[...] += nt(dz_ref[r], up[...])

    hidden(0, wd_ref, wu_ref)
    for copy in down_copies + up_copies:
        copy.wait()
    for r in range(1, 4):
        hidden(r, wd_s.at[r - 1], wu_s.at[r - 1])
    du1 = dh1_ref[...]
    normed = n1_ref[...]
    small_ref[0:1, :] = jnp.sum(du1 * normed, axis=0, keepdims=True)
    small_ref[1:2, :] = jnp.sum(du1, axis=0, keepdims=True)
    dh1 = row_norm_back(du1 * ag_ref[...].astype(F32), normed, r1_ref[...])
    small_ref[2:3, :] = jnp.sum(dh1, axis=0, keepdims=True)
    dh1_ref[...] = dh1
    da_ref[...] = dh1.astype(BF)
    for copy in out_copies:
        copy.wait()
    rows, width = o0.shape
    stat_lane = lax.broadcasted_iota(jnp.int32, (rows, 128), 1)
    for r, o_ref in enumerate((o0, o1, o2, o3)):
        weight = wo_ref[...] if r == 0 else wo_s[r - 1]
        do = nt(da_ref[...], weight).astype(BF)
        do_ref[r] = do
        product = do.astype(F32) * o_ref[...].astype(F32)
        stats = jnp.zeros((rows, 128), F32)
        for h in range(width // HEAD_DIM):
            inner = jnp.sum(
                jnp.where(head_mask(rows, width, h), product, 0.0), axis=-1, keepdims=True
            )
            stats = jnp.where(stat_lane == h, inner, stats)
        delta_ref[r] = jnp.transpose(stats)[:8, :]


def spread_rows(meta, acc, keep_ref, send_ref, lanes=None):
    rows = keep_ref.shape[-2]
    me = meta[1] * 2 + meta[2]
    for j in range(4):
        for side, ref in ((0, keep_ref), (1, send_ref)):
            start = pl.multiple_of((me ^ (2 * j + side)) * rows, 8)
            ref[j, 0] = acc[pl.ds(start, rows), :].astype(BF)


def ffn_weight_kernel(meta, u_ref, df_ref, dz_ref, act_ref, uk_ref, us_ref, dk_ref, ds_ref, ut_s, dt_s, acc):
    @pl.when(pl.program_id(0) == 0)
    def _():
        ut_s[...] = jnp.transpose(u_ref[...])
        dt_s[...] = jnp.transpose(df_ref[...])

    acc[...] = nn(ut_s[...], dz_ref[0])
    spread_rows(meta, acc, uk_ref, us_ref)
    acc[...] = nn(dt_s[...], act_ref[0])
    spread_rows(meta, acc, dk_ref, ds_ref)


def ffn_weight_grads(meta, ulow, dfeed, dz, act):
    rows, dim = ulow.shape
    part = dim // 8
    full = pl.BlockSpec((rows, dim), lambda r, m: (0, 0))
    group = pl.BlockSpec((1, rows, dim), lambda r, m: (r, 0, 0))
    out = pl.BlockSpec((4, 1, part, dim), lambda r, m: (0, r, 0, 0))
    return pl.pallas_call(
        ffn_weight_kernel,
        grid_spec=pltpu.PrefetchScalarGridSpec(
            num_scalar_prefetch=1,
            grid=(4,),
            in_specs=[full, full, group, group],
            out_specs=[out] * 4,
            scratch_shapes=[pltpu.VMEM((dim, rows), BF)] * 2 + [pltpu.VMEM((dim, dim), F32)],
        ),
        out_shape=[jax.ShapeDtypeStruct((4, 4, part, dim), BF)] * 4,
        compiler_params=params(),
        cost_estimate=cost(9),
    )(meta, ulow, dfeed, dz, act)


def attend_back_kernel(
    own, meta, xq_ref, xk_ref, wt_ref, b_ref, do_ref, lse_ref, delta_ref, *refs,
):
    pieces = refs[:8]
    if own:
        dqt_ref, dx_ref, dq_ref, dk_ref, dv_ref, small_ref, w_s, sems, qm_s, dom_s, kt_s = refs[8:]
    else:
        dqt_ref, dx_ref, dk_ref, dv_ref, small_ref, w_s, sems, qm_s, dom_s, kt_s = refs[8:]
    width = wt_ref.shape[1]
    heads = width // HEAD_DIM
    rows, dim = xq_ref.shape
    keys = xk_ref.shape[0]
    scale = HEAD_DIM ** (-0.5)
    quarter_rows = width // 4
    copies = [
        pltpu.make_async_copy(wt_ref.at[m], w_s.at[0, pl.ds(m * width, width), :], sems.at[1, m])
        for m in range(3)
    ]
    copies += place_copies(
        pieces,
        tuple((w_s.at[pl.ds(1, 3)], m * quarter_rows, quarter_rows, m * width) for m in range(3)),
        meta,
        sems.at[0],
    )
    for copy in copies:
        copy.start()
    for copy in copies:
        copy.wait()
    dx = dx_acc = None
    small_ref[...] = jnp.zeros_like(small_ref)
    dx_ref[...] = jnp.zeros_like(dx_ref)
    block = 256

    def group(r, carry):
        bias = b_ref[r].astype(F32)
        q = (nt(xq_ref[...], w_s[r, 0:width, :]) + bias[0:1, :]).astype(BF)
        k = nt(xk_ref[...], w_s[r, width : 2 * width, :]).astype(BF)
        v = (nt(xk_ref[...], w_s[r, 2 * width : 3 * width, :]) + bias[1:2, :]).astype(BF)
        do = do_ref[r]
        zero = jnp.zeros_like(q)
        for h in range(heads):
            mask = head_mask(rows, width, h)
            qm_s[h] = jnp.where(mask, q, zero)
            dom_s[h] = jnp.where(mask, do, zero)
        kt_s[...] = jnp.transpose(k)
        dqt = [None] * heads
        for kb in range(keys // block):
            span = slice(kb * block, (kb + 1) * block)
            dk = dv = None
            for h in range(heads):
                s = nt(k[span, :], qm_s[h])
                p = jnp.exp2(s * (scale * LOG2E) - lse_ref[r, h : h + 1, :])
                dp = nt(v[span, :], dom_s[h])
                ds = (p * (dp - delta_ref[r, h : h + 1, :])).astype(BF)
                dv_part = nn(p.astype(BF), dom_s[h])
                dk_part = nn(ds, qm_s[h])
                dq_part = nn(kt_s[h * HEAD_DIM : (h + 1) * HEAD_DIM, span], ds)
                dv = dv_part if dv is None else dv + dv_part
                dk = dk_part if dk is None else dk + dk_part
                dqt[h] = dq_part if dqt[h] is None else dqt[h] + dq_part
            dk_low = (dk * scale).astype(BF)
            dv_low = dv.astype(BF)
            dk_ref[r, span, :] = dk_low
            dv_ref[r, span, :] = dv_low
            small_ref[r, 1:2, :] += jnp.sum(dv_low.astype(F32), axis=0, keepdims=True)
            dx_ref[span, :] += (
                nn(dk_low, w_s[r, width : 2 * width, :]) + nn(dv_low, w_s[r, 2 * width : 3 * width, :])
            ).astype(dx_ref.dtype)
        whole = jnp.concatenate(dqt, axis=0)
        if own:
            dq_low = (jnp.transpose(whole + dqt_ref[r]) * scale).astype(BF)
            dq_ref[r] = dq_low
            small_ref[r, 0:1, :] = jnp.sum(dq_low.astype(F32), axis=0, keepdims=True)
            dx_ref[...] += nn(dq_low, w_s[r, 0:width, :])
        else:
            dqt_ref[r] = whole
        return carry

    lax.fori_loop(0, 4, group, 0)


def attend_back(meta, own, inputs, wt, bias, do, lse, delta, pieces, dqt=None):
    rows, width = do.shape[1:]
    dim = inputs.shape[1]
    other = 0 if own else 1
    outs = [
        jax.ShapeDtypeStruct((rows, dim), F32),
        jax.ShapeDtypeStruct((4, rows, width), BF),
        jax.ShapeDtypeStruct((4, rows, width), BF),
        jax.ShapeDtypeStruct((4, 2, width), F32),
    ]
    partial_shape = jax.ShapeDtypeStruct((4, width, rows), F32)
    if own:
        outs = outs[:1] + [jax.ShapeDtypeStruct((4, rows, width), BF)] + outs[1:]
    else:
        outs = [partial_shape] + outs
    extra = [dqt] if own else []
    return pl.pallas_call(
        partial(attend_back_kernel, own),
        grid_spec=pltpu.PrefetchScalarGridSpec(
            num_scalar_prefetch=1,
            grid=(1,),
            in_specs=[
                pl.BlockSpec((rows, dim), lambda i, m: (m[0], 0)),
                pl.BlockSpec((rows, dim), lambda i, m: (m[0] ^ other, 0)),
                ANY,
                VM,
                VM,
                VM,
                VM,
            ]
            + [ANY] * 8
            + [VM] * len(extra),
            out_specs=[VM] * len(outs),
            scratch_shapes=[
                pltpu.VMEM((4, 3 * width, dim), BF),
                pltpu.SemaphoreType.DMA((2, 24)),
                pltpu.VMEM((width // HEAD_DIM, rows, width), BF),
                pltpu.VMEM((width // HEAD_DIM, rows, width), BF),
                pltpu.VMEM((width, rows), BF),
            ],
        ),
        out_shape=outs,
        compiler_params=params(),
        cost_estimate=cost(14),
    )(meta, inputs, inputs, wt, bias, do, lse, delta, *pieces, *extra)


def attend_weight_kernel(
    meta, xq_ref, xk_ref, da_ref, dq_ref, dko_ref, dvo_ref, dkp_ref, dvp_ref, o_ref, keep_ref, send_ref, xq_s, xk_s, da_s, acc
):
    @pl.when(pl.program_id(0) == 0)
    def _():
        xq_s[...] = jnp.transpose(xq_ref[...])
        xk_s[...] = jnp.transpose(xk_ref[...])
        da_s[...] = jnp.transpose(da_ref[...])

    acc[...] = jnp.concatenate(
        [
            nn(xq_s[...], dq_ref[0]),
            nn(xq_s[...], dko_ref[0]) + nn(xk_s[...], dkp_ref[0]),
            nn(xq_s[...], dvo_ref[0]) + nn(xk_s[...], dvp_ref[0]),
            nn(da_s[...], o_ref[0]),
        ],
        axis=1,
    )
    spread_rows(meta, acc, keep_ref, send_ref)


def attend_weight_grads(meta, inputs, dattn, dq, dk_own, dv_own, dk_other, dv_other, mixed):
    rows, dim = dattn.shape
    width = dq.shape[2]
    part = dim // 8
    group = pl.BlockSpec((1, rows, width), lambda r, m: (r, 0, 0))
    out = pl.BlockSpec((4, 1, part, dim), lambda r, m: (0, r, 0, 0))
    return pl.pallas_call(
        attend_weight_kernel,
        grid_spec=pltpu.PrefetchScalarGridSpec(
            num_scalar_prefetch=1,
            grid=(4,),
            in_specs=[
                pl.BlockSpec((rows, dim), lambda r, m: (m[0], 0)),
                pl.BlockSpec((rows, dim), lambda r, m: (m[0] ^ 1, 0)),
                pl.BlockSpec((rows, dim), lambda r, m: (0, 0)),
            ]
            + [group] * 6,
            out_specs=[out] * 2,
            scratch_shapes=[pltpu.VMEM((dim, rows), BF)] * 3 + [pltpu.VMEM((dim, dim), F32)],
        ),
        out_shape=[jax.ShapeDtypeStruct((4, 4, part, dim), BF)] * 2,
        compiler_params=params(),
        cost_estimate=cost(8),
    )(meta, inputs, inputs, dattn, dq, dk_own, dv_own, dk_other, dv_other, mixed)


def over_z(x, r):
    return lax.ppermute(x, "tensor", [(i, i ^ r) for i in range(4)])


def over_dp(x, offset, size):
    return lax.ppermute(x, "dp", [(i, i ^ offset) for i in range(size)])


def gather_pieces(piece, dp):
    remote = jnp.stack([over_z(piece, r) for r in (1, 2, 3)])
    own = [remote] + [over_dp(remote, 2 * j, dp) for j in (1, 2, 3)]
    return own + [over_dp(p, 1, dp) for p in own]


def add_low(*terms):
    total = terms[0].astype(F32)
    for term in terms[1:]:
        total = total + term.astype(F32)
    return total.astype(BF)


def reduce_weight(keep, send, dp, me):
    if dp == 8:
        other = over_dp(send, 1, dp)
        sums = [add_low(keep[j], other[j]) for j in range(4)]
        arrived = [over_dp(sums[j], 2 * j, dp) for j in (1, 2, 3)]
        mine = add_low(sums[0], *arrived)
    else:
        both = jnp.stack([keep, send], 1).reshape((8,) + keep.shape[1:])
        both = jnp.take(both, jnp.arange(8) ^ (me % 8), axis=0)
        both = both.transpose(0, 2, 1, 3).reshape(-1, 4, keep.shape[3])
        mine = lax.psum_scatter(both.astype(F32), "dp", scatter_dimension=0, tiled=True)
        mine = mine.transpose(1, 0, 2).astype(BF)
    total = mine[0].astype(F32)
    for r in (1, 2, 3):
        total = total + over_z(mine[r], r).astype(F32)
    return total


def sum_over_dp(x, dp):
    offset = 1
    while offset < dp:
        x = x + over_dp(x, offset, dp)
        offset *= 2
    return x


def per_device(
    dp,
    inputs,
    qkv_weight,
    qv_bias,
    out_weight,
    out_bias,
    attn_gain,
    attn_shift,
    up_weight,
    up_bias,
    down_weight,
    down_bias,
    ffn_gain,
    ffn_shift,
    keep_mask,
    cotangent,
):
    tokens, dim = inputs.shape
    length = tokens // keep_mask.shape[0]
    width = qkv_weight.shape[2]
    rows = tokens // 4
    z = lax.axis_index("tensor")
    me = lax.axis_index("dp")
    core = me % 2
    quarter = (me // 2) % 4
    keep_value = lax.dynamic_index_in_dim(keep_mask, z // 2, 0, keepdims=False)
    meta = jnp.stack([z, quarter, core, keep_value]).astype(jnp.int32)
    lanes = dim // 2
    row = lambda v: v.reshape(1, dim)

    def piece_of(weight):
        part = weight.shape[0] // 4
        return lax.dynamic_slice(weight, (quarter * part, core * lanes), (part, lanes))

    up_out = gather_pieces(jnp.concatenate([piece_of(up_weight), piece_of(out_weight)]), dp)
    down = gather_pieces(piece_of(down_weight), dp)
    wt = qkv_weight.transpose(0, 2, 1)
    part = width // 4
    wt_piece = lax.dynamic_slice(wt, (0, quarter * part, core * lanes), (3, part, lanes))
    qkv = gather_pieces(wt_piece.reshape(3 * part, lanes), dp)
    bias_pack = jnp.concatenate([row(up_bias), jnp.pad(qv_bias, ((0, 0), (0, dim - width)))])
    bias_packs = jnp.stack([bias_pack] + [over_z(bias_pack, r) for r in (1, 2, 3)])
    up_bias_all = bias_packs[:, 0]
    qv_bias_all = bias_packs[:, 1:3, :width]

    far0, far1, far_l0, far_l1 = attend(meta, inputs, qkv_weight, qv_bias, length, 1)
    o2, l2 = over_z(far0, 2), over_z(far_l0, 2)
    o3, l3 = over_z(far1, 3), over_z(far_l1, 3)
    o0, near, l0, near_l = attend(meta, inputs, qkv_weight, qv_bias, length, 0)
    o1, l1 = over_z(near, 1), over_z(near_l, 1)
    lse = jnp.stack([l0, l1, l2, l3])

    own_rows = pl.BlockSpec((rows, dim), lambda i, m: (m[0], 0))
    hidden_low = jax.ShapeDtypeStruct((4, rows, dim), BF)
    wide = jax.ShapeDtypeStruct((rows, dim), F32)
    low = jax.ShapeDtypeStruct((rows, dim), BF)
    out_scratch = pltpu.VMEM((3, width, dim), BF)
    square = pltpu.VMEM((3, dim, dim), BF)

    n1, r1, ulow, act, der = pl.pallas_call(
        up_kernel,
        grid_spec=pltpu.PrefetchScalarGridSpec(
            num_scalar_prefetch=1,
            grid=(1,),
            in_specs=[own_rows] + [VM] * 10 + [ANY] * 8,
            out_specs=[VM] * 5,
            scratch_shapes=[out_scratch, square, pltpu.SemaphoreType.DMA((2, 8))],
        ),
        out_shape=[wide, jax.ShapeDtypeStruct((rows, 1), F32), low, hidden_low, hidden_low],
        compiler_params=params(),
        cost_estimate=cost(12),
    )(
        meta, inputs, o0, o1, o2, o3, row(out_bias), row(attn_gain), row(attn_shift), up_bias_all,
        out_weight, up_weight, *up_out,
    )

    outputs_own, dh2, dfeed, small_down = pl.pallas_call(
        down_kernel,
        grid_spec=pltpu.PrefetchScalarGridSpec(
            num_scalar_prefetch=1,
            grid=(1,),
            in_specs=[VM] * 7 + [own_rows] * 2 + [VM] + [ANY] * 8,
            out_specs=[VM] * 4,
            scratch_shapes=[square, pltpu.SemaphoreType.DMA((8,))],
        ),
        out_shape=[low, wide, low, jax.ShapeDtypeStruct((8, dim), F32)],
        compiler_params=params(),
        cost_estimate=cost(6),
    )(
        meta, n1, row(attn_gain), row(attn_shift), row(down_bias), row(ffn_gain), row(ffn_shift), act,
        inputs, cotangent, down_weight, *down,
    )

    dz, dh1, dattn, do, delta, small_up = pl.pallas_call(
        ffn_back_kernel,
        grid_spec=pltpu.PrefetchScalarGridSpec(
            num_scalar_prefetch=1,
            grid=(1,),
            in_specs=[VM] * 13 + [ANY] * 16,
            out_specs=[VM] * 6,
            scratch_shapes=[square, square, out_scratch, pltpu.SemaphoreType.DMA((3, 8))],
        ),
        out_shape=[
            hidden_low,
            wide,
            low,
            jax.ShapeDtypeStruct((4, rows, width), BF),
            jax.ShapeDtypeStruct((4, 8, rows), F32),
            jax.ShapeDtypeStruct((16, dim), F32),
        ],
        compiler_params=params(),
        cost_estimate=cost(10),
    )(
        meta, dfeed, dh2, der, n1, r1, row(attn_gain), o0, o1, o2, o3, down_weight, up_weight, out_weight,
        *down, *up_out,
    )

    outputs_parts = [outputs_own] + [over_z(outputs_own, r) for r in (1, 2, 3)]

    dqt, dx_other, dk_other, dv_other, small_other = attend_back(
        meta, False, inputs, wt, qv_bias_all, do, lse, delta, qkv
    )
    dx_arrived = over_z(dx_other.astype(BF), 1)
    up_keep, up_send, down_keep, down_send = ffn_weight_grads(meta, ulow, dfeed, dz, act)
    dx_own, dq, dk_own, dv_own, small_own = attend_back(
        meta, True, inputs, wt, qv_bias_all, do, lse, delta, qkv, dqt
    )
    cot_own = lax.dynamic_slice(cotangent, (z * rows, 0), (rows, dim))
    grad_own = jnp.where(keep_value > 0, (dh1 + (dx_own + dx_arrived.astype(F32))).astype(BF), cot_own)
    grad_parts = [grad_own] + [over_z(grad_own, r) for r in (1, 2, 3)]
    qkvo_keep, qkvo_send = attend_weight_grads(
        meta, inputs, dattn, dq, dk_own, dv_own, dk_other, dv_other, jnp.stack([o0, o1, o2, o3])
    )

    grad_up = reduce_weight(up_keep, up_send, dp, me)
    grad_down = reduce_weight(down_keep, down_send, dp, me).T
    grad_qkvo = reduce_weight(qkvo_keep, qkvo_send, dp, me)
    grad_qkv = jnp.stack([grad_qkvo[:, m * width : (m + 1) * width] for m in range(3)])
    grad_out = grad_qkvo[:, 3 * width :].T

    small = sum_over_dp(jnp.concatenate([small_down[:3], small_up[:3], small_up[8:12]]), dp)
    same = small[:6]
    for r in (1, 2):
        same = same + over_z(same, r)
    grad_up_bias = small[6]
    for r in (1, 2, 3):
        grad_up_bias = grad_up_bias + over_z(small[6 + r], r)
    qv = sum_over_dp(small_own + small_other, dp)
    grad_qv_bias = qv[0]
    for r in (1, 2, 3):
        grad_qv_bias = grad_qv_bias + over_z(qv[r], r)

    outputs = jnp.zeros((tokens, dim), BF)
    grad_inputs = jnp.zeros((tokens, dim), F32)
    for r in range(4):
        outputs = lax.dynamic_update_slice(outputs, outputs_parts[r], ((z ^ r) * rows, 0))
        grad_inputs = lax.dynamic_update_slice(
            grad_inputs, grad_parts[r].astype(F32), ((z ^ r) * rows, 0)
        )
    return (
        outputs,
        grad_inputs,
        grad_qkv,
        grad_qv_bias,
        grad_out,
        same[5],
        same[3],
        same[4],
        grad_up,
        grad_up_bias,
        grad_down,
        same[2],
        same[0],
        same[1],
    )


def solution(mesh):
    placed = (
        P("dp", None),
        P(None, None, "tensor"),
        P(None, "tensor"),
        P("tensor", None),
        P(),
        P(),
        P(),
        P(None, "tensor"),
        P("tensor"),
        P("tensor", None),
        P(),
        P(),
        P(),
        P("dp"),
        P("dp", None),
    )
    return jax.shard_map(
        partial(per_device, mesh.shape["dp"]),
        mesh=mesh,
        in_specs=placed,
        out_specs=(
            P("dp", None),
            P("dp", None),
            P(None, "dp", "tensor"),
            P(None, "tensor"),
            P("tensor", "dp"),
            P(),
            P(),
            P(),
            P("dp", "tensor"),
            P("tensor"),
            P("tensor", "dp"),
            P(),
            P(),
            P(),
        ),
        check_vma=False,
    )
```

time: 840 us -> 545 us (0.65)
  waiting for transfers between devices: 558 us -> 235 us
  matrix products: 130 us -> 0 us
  starting transfers between devices: 0.58 us -> 130 us
  Pallas kernels: 0 us -> 127 us
  other arithmetic: 62.9 us -> 17.5 us
  blocking collectives: 24.7 us -> 0 us
  local copies, waits for them, and re-layouts: 43.4 us -> 23 us
  between operations: 15.5 us -> 2.54 us
    psum x4 -> x0, waiting for transfers between devices: 473 us -> none  [the longest x1 124 us: per_device(): lax.psum(jnp.dot(mixed_low, out_weight, preferred_element_type=jnp.float3...]
    ppermute x0 -> x81, waiting for transfers between devices: none -> 235 us  [the longest x42 155 us: over_z(): return lax.ppermute(x, 'tensor', [(i, i ^ r) for i in range(4)])]
    ppermute x0 -> x81, starting transfers between devices: none -> 130 us  [the longest x42 98.1 us: over_z(): return lax.ppermute(x, 'tensor', [(i, i ^ r) for i in range(4)])]
    pallas_call x0 -> x9, Pallas kernels: none -> 127 us  [the longest x2 43.5 us: attend_back(): pl.pallas_call(partial(attend_back_kernel, own), grid_spec=pltpu.Prefetch...]
    dot_general x45 -> x0, matrix products: 125 us -> none  [the longest x1 18.7 us: per_device(): jnp.dot(first_low, up_weight, preferred_element_type=jnp.float32)]
    reduce_scatter x2 -> x0, waiting for transfers between devices: 84.6 us -> none  [the longest x1 46.4 us: per_device(): lax.psum_scatter(grad_up, 'dp', scatter_dimension=0, tiled=True)]
    reduce_sum x13 -> x0, other arithmetic: 42.7 us -> none  [the longest x1 9.41 us: per_device(): grad_attn_gain = jnp.sum(grad_first * first_normed, axis=0)]
    psum x1 -> x0, blocking collectives: 24.7 us -> none  [per_device(): lax.psum((grad_qv_bias, grad_out_bias, grad_attn_gain, grad_attn_shift, g...]
  transfers between devices with their start and end apart: 8 -> 81, of which waited for: 6 -> 23; matrix products, arithmetic and copies ran while one was open for 12% -> 6% of each run, Pallas kernels for 0% -> 24%
where the time goes in v1:
time: 545 us; the launch traced here: 534 us
  waiting for transfers between devices  235 us (43%)
  starting transfers between devices  130 us (24%)
  Pallas kernels  127 us (23%)
  local copies, waits for them, and re-layouts  23 us (4%)
  other arithmetic  17.5 us (3%)
    ppermute x42, waiting for transfers between devices, over_z(): return lax.ppermute(x, 'tensor', [(i, i ^ r) for i in range(4)])  155 us
    ppermute x42, starting transfers between devices, over_z(): return lax.ppermute(x, 'tensor', [(i, i ^ r) for i in range(4)])  98.1 us
    ppermute x39, waiting for transfers between devices, over_dp(): return lax.ppermute(x, 'dp', [(i, i ^ offset) for i in range(size)])  79.5 us
    pallas_call x2, Pallas kernels, attend_back(): pl.pallas_call(partial(attend_back_kernel, own), grid_spec=pltpu.Prefetch...  43.5 us
    ppermute x39, starting transfers between devices, over_dp(): return lax.ppermute(x, 'dp', [(i, i ^ offset) for i in range(size)])  32 us
    pallas_call x2, Pallas kernels, attend(): pl.pallas_call(attend_kernel, grid_spec=pltpu.PrefetchScalarGridSpec(num_...  18.5 us
    pallas_call x1, Pallas kernels, per_device(): pl.pallas_call(ffn_back_kernel, grid_spec=pltpu.PrefetchScalarGridSpec(nu...  15.5 us
    pallas_call x1, Pallas kernels, per_device(): pl.pallas_call(up_kernel, grid_spec=pltpu.PrefetchScalarGridSpec(num_scal...  14.6 us
  transfers between devices with their start and end apart: 81, of which 23 were waited for; matrix products, arithmetic and copies ran while one was open for 6% of the time, Pallas kernels for 24%

profile of v1, /device:TPU:0, one launch (start us, length us, event | category | flops | bytes accessed | tf_op | source)
XLA Modules:
  0.0 534.3 jit_solution(4835524223569972513)
XLA Ops:
  2.0 3.1 collective-permute-start.3
  11.9 9.3 %shard_map.254 = (bf16[512,192]{1,0:T(8,128)(2,1)}, bf16[512,192]{1,0:T(8,128)(2,1)}, f32[8,512]{1,0:T(8,128)}, f32[8,512]{1,0:T(8,128)}) custom-call(s32[4]{0:T(128)} %pad_add_fusion.meta, bf16[2048,768]{1,0:T(8,128)(2,1)} %xk_ref.5, bf16[3,768,192]{2,1,0:T(8,128)(2,1)} %copy.32.w_ref, bf16[2,192]{1,0:T(2,128)(2,1)} %b_ref.3), custom_call_target="tpu_custom_call" | custom-call | flops 7200000000 | bytes 1024 | tf_op jit(solution)/shard_map/pallas_call | solution.py:127
  22.0 9.3 %shard_map.255 = (bf16[512,192]{1,0:T(8,128)(2,1)}, bf16[512,192]{1,0:T(8,128)(2,1)}, f32[8,512]{1,0:T(8,128)}, f32[8,512]{1,0:T(8,128)}) custom-call(s32[4]{0:T(128)} %pad_add_fusion.meta, bf16[2048,768]{1,0:T(8,128)(2,1)} %xk_ref.5, bf16[3,768,192]{2,1,0:T(8,128)(2,1)} %copy.32.w_ref, bf16[2,192]{1,0:T(2,128)(2,1)} %b_ref.3), custom_call_target="tpu_custom_call" | custom-call | flops 7200000000 | bytes 1024 | tf_op jit(solution)/shard_map/pallas_call | solution.py:127
  31.3 4.0 collective-permute-start.30
  39.6 3.8 collective-permute-start.34
  44.1 7.5 %collective-permute-done.31 = f32[8,512]{1,0:T(8,128)S(1)} collective-permute-done((f32[8,512]{1,0:T(8,128)}, f32[8,512]{1,0:T(8,128)S(1)}, u32[]{:S(2)}, u32[]{:S(2)}) %collective-permute-start.31) | collective-permute-done | bytes 16416 | tf_op jit(solution)/shard_map/ppermute | solution.py:489
  58.5 18.3 %collective-permute-done.17 = bf16[192,384]{1,0:T(8,128)(2,1)S(1)} collective-permute-done((bf16[192,384]{1,0:T(8,128)(2,1)S(1)}, bf16[192,384]{1,0:T(8,128)(2,1)S(1)}, u32[]{:S(2)}, u32[]{:S(2)}) %collective-permute-start.17) | collective-permute-done | bytes 147488 | tf_op jit(solution)/shard_map/ppermute | solution.py:489
  88.7 12.0 %collective-permute-done.1.o2 = bf16[512,192]{1,0:T(8,128)(2,1)S(1)} collective-permute-done((bf16[512,192]{1,0:T(8,128)(2,1)S(1)}, bf16[512,192]{1,0:T(8,128)(2,1)S(1)}, u32[]{:S(2)}, u32[]{:S(2)}) %collective-permute-start.1) | collective-permute-done | bytes 196640 | tf_op jit(solution)/shard_map/ppermute | solution.py:489
  105.9 16.2 %collective-permute-done.19.p1.d1 = bf16[3,192,384]{2,1,0:T(8,128)(2,1)} collective-permute-done((bf16[3,192,384]{2,1,0:T(8,128)(2,1)S(1)}, bf16[3,192,384]{2,1,0:T(8,128)(2,1)}, u32[]{:S(2)}, u32[]{:S(2)}) %collective-permute-start.19) | collective-permute-done | bytes 442400 | tf_op jit(solution)/shard_map/ppermute | solution.py:493
  122.7 2.8 collective-permute-done.10.p2
  126.0 6.8 %collective-permute-done.20.p2.d2 = bf16[3,192,384]{2,1,0:T(8,128)(2,1)} collective-permute-done((bf16[3,192,384]{2,1,0:T(8,128)(2,1)S(1)}, bf16[3,192,384]{2,1,0:T(8,128)(2,1)}, u32[]{:S(2)}, u32[]{:S(2)}) %collective-permute-start.20) | collective-permute-done | bytes 442400 | tf_op jit(solution)/shard_map/ppermute | solution.py:493
  140.6 3.9 collective-permute-done.21.p3.d3
  148.8 14.6 %shard_map.256 = (f32[512,768]{1,0:T(8,128)}, f32[512,1]{1,0:T(8,128)}, bf16[512,768]{1,0:T(8,128)(2,1)}, bf16[4,512,768]{2,1,0:T(8,128)(2,1)}, bf16[4,512,768]{2,1,0:T(8,128)(2,1)}) custom-call(s32[4]{0:T(128)} %pad_add_fusion.meta, bf16[2048,768]{1,0:T(8,128)(2,1)} %xk_ref.5, bf16[512,192]{1,0:T(8,128)(2,1)} %get-tuple-element.53.o0, ...), custom_call_target="tpu_custom_call" | custom-call | flops 10800000000 | bytes 1024 | tf_op jit(solution)/shard_map/pallas_call | solution.py:595
  164.6 11.2 %shard_map.257 = (bf16[512,768]{1,0:T(8,128)(2,1)}, f32[512,768]{1,0:T(8,128)}, bf16[512,768]{1,0:T(8,128)(2,1)}, f32[8,768]{1,0:T(8,128)}) custom-call(s32[4]{0:T(128)} %pad_add_fusion.meta, f32[512,768]{1,0:T(8,128)} %get-tuple-element.57.n1_ref, bf16[1,768]{1,0:T(2,128)(2,1)} %reshape.118.ag_ref, bf16[1,768]{1,0:T(2,128)(2,1)} %reshape.119.as_ref, ...), custom_call_target="tpu_custom_call" | custom-call | flops 5400000000 | bytes 1024 | tf_op jit(solution)/shard_map/pallas_call | solution.py:612
  175.8 15.5 %shard_map.258 = (bf16[4,512,768]{2,1,0:T(8,128)(2,1)}, f32[512,768]{1,0:T(8,128)}, bf16[512,768]{1,0:T(8,128)(2,1)}, bf16[4,512,192]{2,1,0:T(8,128)(2,1)}, f32[4,8,512]{2,1,0:T(8,128)}, /*index=5*/f32[16,768]{1,0:T(8,128)}) custom-call(s32[4]{0:T(128)} %pad_add_fusion.meta, bf16[512,768]{1,0:T(8,128)(2,1)} %get-tuple-element.60.df_ref, ...), custom_call_target="tpu_custom_call" | custom-call | flops 8999999488 | bytes 1024 | tf_op jit(solution)/shard_map/pallas_call | solution.py:629
  194.2 21.3 %shard_map.259 = (f32[4,192,512]{2,1,0:T(8,128)}, f32[512,768]{1,0:T(8,128)}, bf16[4,512,192]{2,1,0:T(8,128)(2,1)}, bf16[4,512,192]{2,1,0:T(8,128)(2,1)}, f32[4,2,192]{2,1,0:T(2,128)}) custom-call(s32[4]{0:T(128)} %pad_add_fusion.meta, bf16[2048,768]{1,0:T(8,128)(2,1)} %xk_ref.5, bf16[2048,768]{1,0:T(8,128)(2,1)} %xk_ref.5, bf16[3,192,768]{2,1,0:T(8,128)(2,1)} %bitcast.123, ...), custom_call_target="tpu_custom_call" | custom-call | flops 12600000512 | bytes 1024 | tf_op jit(solution)/shard_map/pallas_call | solution.py:410
  215.6 22.2 %shard_map.260 = (f32[512,768]{1,0:T(8,128)}, bf16[4,512,192]{2,1,0:T(8,128)(2,1)}, bf16[4,512,192]{2,1,0:T(8,128)(2,1)}, bf16[4,512,192]{2,1,0:T(8,128)(2,1)}, f32[4,2,192]{2,1,0:T(2,128)}) custom-call(s32[4]{0:T(128)} %pad_add_fusion.meta, bf16[2048,768]{1,0:T(8,128)(2,1)} %xk_ref.5, bf16[2048,768]{1,0:T(8,128)(2,1)} %xk_ref.5, ...), custom_call_target="tpu_custom_call" | custom-call | flops 12600000512 | bytes 1024 | tf_op jit(solution)/shard_map/pallas_call | solution.py:410
  249.6 3.8 collective-permute-start.57
  257.9 11.7 %shard_map.262 = (bf16[4,4,96,768]{3,2,1,0:T(8,128)(2,1)}, bf16[4,4,96,768]{3,2,1,0:T(8,128)(2,1)}, bf16[4,4,96,768]{3,2,1,0:T(8,128)(2,1)}, bf16[4,4,96,768]{3,2,1,0:T(8,128)(2,1)}) custom-call(s32[4]{0:T(128)} %pad_add_fusion.meta, bf16[512,768]{1,0:T(8,128)(2,1)} %get-tuple-element.86.u_ref, bf16[512,768]{1,0:T(8,128)(2,1)} %get-tuple-element.60.df_ref, ...), custom_call_target="tpu_custom_call" | custom-call | flops 8099999744 | bytes 1024 | tf_op jit(solution)/shard_map/pallas_call | solution.py:298
  274.8 11.5 %shard_map.261 = (bf16[4,4,96,768]{3,2,1,0:T(8,128)(2,1)}, bf16[4,4,96,768]{3,2,1,0:T(8,128)(2,1)}) custom-call(s32[4]{0:T(128)} %pad_add_fusion.meta, bf16[2048,768]{1,0:T(8,128)(2,1)} %xk_ref.5, bf16[2048,768]{1,0:T(8,128)(2,1)} %xk_ref.5, bf16[512,768]{1,0:T(8,128)(2,1)} %get-tuple-element.74.da_ref, bf16[4,512,192]{2,1,0:T(8,128)(2,1)} %get-tuple-element.75.dq_ref, ...), custom_call_target="tpu_custom_call" | custom-call | flops 7200000000 | bytes 1024 | tf_op jit(solution)/shard_map/pallas_call | solution.py:468
  286.2 34.6 %collective-permute-done.62 = f32[6,768]{1,0:T(8,128)S(1)} collective-permute-done((f32[6,768]{1,0:T(8,128)S(1)}, f32[6,768]{1,0:T(8,128)S(1)}, u32[]{:S(2)}, u32[]{:S(2)}) %collective-permute-start.62) | collective-permute-done | bytes 18464 | tf_op jit(solution)/shard_map/ppermute | solution.py:489
  322.3 3.9 collective-permute-done.73
  327.8 3.5 collective-permute-done.63
  340.2 13.5 %collective-permute-done.28 = bf16[512,768]{1,0:T(8,128)(2,1)S(1)} collective-permute-done((bf16[512,768]{1,0:T(8,128)(2,1)}, bf16[512,768]{1,0:T(8,128)(2,1)S(1)}, u32[]{:S(2)}, u32[]{:S(2)}) %collective-permute-start.28) | collective-permute-done | bytes 786464 | tf_op jit(solution)/shard_map/ppermute | solution.py:489
  353.7 11.7 %collective-permute-start.44 = (bf16[512,768]{1,0:T(8,128)(2,1)S(1)}, bf16[512,768]{1,0:T(8,128)(2,1)S(1)}, u32[]{:S(2)}, u32[]{:S(2)}) collective-permute-start(bf16[512,768]{1,0:T(8,128)(2,1)S(1)} %get-tuple-element.131), channel_id=1, source_target_pairs={{0,2},{1,3},{2,0},{3,1},{4,6},{5,7},{6,4},{7,5},{8,10},{9,11},{10,... | collective-permute-start | bytes 2359304 | tf_op jit(solution)/shard_map/ppermute | solution.py:489
  372.1 44.2 %collective-permute-done.44 = bf16[512,768]{1,0:T(8,128)(2,1)S(1)} collective-permute-done((bf16[512,768]{1,0:T(8,128)(2,1)S(1)}, bf16[512,768]{1,0:T(8,128)(2,1)S(1)}, u32[]{:S(2)}, u32[]{:S(2)}) %collective-permute-start.44) | collective-permute-done | bytes 786464 | tf_op jit(solution)/shard_map/ppermute | solution.py:489
  424.1 27.6 %collective-permute-done.76 = bf16[4,96,768]{2,1,0:T(8,128)(2,1)S(1)} collective-permute-done((bf16[4,96,768]{2,1,0:T(8,128)(2,1)S(1)}, bf16[4,96,768]{2,1,0:T(8,128)(2,1)S(1)}, u32[]{:S(2)}, u32[]{:S(2)}) %collective-permute-start.76) | collective-permute-done | bytes 589856 | tf_op jit(solution)/shard_map/ppermute | solution.py:493
  456.8 16.0 %collective-permute-done.66 = bf16[4,96,768]{2,1,0:T(8,128)(2,1)S(1)} collective-permute-done((bf16[4,96,768]{2,1,0:T(8,128)(2,1)S(1)}, bf16[4,96,768]{2,1,0:T(8,128)(2,1)S(1)}, u32[]{:S(2)}, u32[]{:S(2)}) %collective-permute-start.66) | collective-permute-done | bytes 589856 | tf_op jit(solution)/shard_map/ppermute | solution.py:493
  472.8 15.7 %collective-permute-start.78 = (bf16[96,768]{1,0:T(8,128)(2,1)S(1)}, bf16[96,768]{1,0:T(8,128)(2,1)S(1)}, u32[]{:S(2)}, u32[]{:S(2)}) collective-permute-start(bf16[96,768]{1,0:T(8,128)(2,1)S(1)} %get-tuple-element.141), channel_id=1, source_target_pairs={{0,1},{1,0},{2,3},{3,2},{4,5},{5,4},{6,7},{7,6},{8,9},{9,8},{10,11... | collective-permute-start | bytes 442376 | tf_op jit(solution)/shard_map/ppermute | solution.py:489
  492.1 17.3 %collective-permute-start.68 = (bf16[96,768]{1,0:T(8,128)(2,1)S(1)}, bf16[96,768]{1,0:T(8,128)(2,1)S(1)}, u32[]{:S(2)}, u32[]{:S(2)}) collective-permute-start(bf16[96,768]{1,0:T(8,128)(2,1)S(1)} %get-tuple-element.144), channel_id=1, source_target_pairs={{0,1},{1,0},{2,3},{3,2},{4,5},{5,4},{6,7},{7,6},{8,9},{9,8},{10,11... | collective-permute-start | bytes 442376 | tf_op jit(solution)/shard_map/ppermute | solution.py:489
  515.2 4.9 collective-permute-done.50
  521.7 9.7 %collective-permute-done.51 = bf16[96,768]{1,0:T(8,128)(2,1)S(1)} collective-permute-done((bf16[96,768]{1,0:T(8,128)(2,1)S(1)}, bf16[96,768]{1,0:T(8,128)(2,1)S(1)}, u32[]{:S(2)}, u32[]{:S(2)}) %collective-permute-start.51) | collective-permute-done | bytes 147488 | tf_op jit(solution)/shard_map/ppermute | solution.py:489
  (301 shorter events, 120.5 us)
Async XLA Ops:
  2.0 36.9 %collective-permute-start.3 = (bf16[3,768]{1,0:T(4,128)(2,1)S(1)}, bf16[3,768]{1,0:T(4,128)(2,1)S(1)}, u32[]{:S(2)}, u32[]{:S(2)}) collective-permute-start(bf16[3,768]{1,0:T(4,128)(2,1)S(1)} %get-tuple-element.158), channel_id=1, source_target_pairs={{0,1},{1,0},{2,3},{3,2},{4,5},{5,4},{6,7},{7,6},{8,9},{9,8},{10,11... | collective-permute-start | bytes 13832 | tf_op jit(solution)/shard_map/ppermute | solution.py:489
  5.1 33.9 %collective-permute-start.4 = (bf16[3,768]{1,0:T(4,128)(2,1)S(1)}, bf16[3,768]{1,0:T(4,128)(2,1)S(1)}, u32[]{:S(2)}, u32[]{:S(2)}) collective-permute-start(bf16[3,768]{1,0:T(4,128)(2,1)S(1)} %get-tuple-element.158), channel_id=1, source_target_pairs={{0,2},{1,3},{2,0},{3,1},{4,6},{5,7},{6,4},{7,5},{8,10},{9,11},{10,... | collective-permute-start | bytes 13832 | tf_op jit(solution)/shard_map/ppermute | solution.py:489
  7.7 31.9 %collective-permute-start.5 = (bf16[3,768]{1,0:T(4,128)(2,1)S(1)}, bf16[3,768]{1,0:T(4,128)(2,1)S(1)}, u32[]{:S(2)}, u32[]{:S(2)}) collective-permute-start(bf16[3,768]{1,0:T(4,128)(2,1)S(1)} %get-tuple-element.158), channel_id=1, source_target_pairs={{0,3},{1,2},{2,1},{3,0},{4,7},{5,6},{6,5},{7,4},{8,11},{9,10},{10,... | collective-permute-start | bytes 13832 | tf_op jit(solution)/shard_map/ppermute | solution.py:489
  51.6 28.9 %collective-permute-start.6 = (bf16[240,384]{1,0:T(8,128)(2,1)S(1)}, bf16[240,384]{1,0:T(8,128)(2,1)S(1)}, u32[]{:S(2)}, u32[]{:S(2)}) collective-permute-start(bf16[240,384]{1,0:T(8,128)(2,1)S(1)} %pad_maximum_fusion.5), channel_id=1, source_target_pairs={{0,1},{1,0},{2,3},{3,2},{4,5},{5,4},{6,7},{7,6},{8,9},{9,8},{10,11... | collective-permute-start | bytes 552968 | tf_op jit(solution)/shard_map/ppermute | solution.py:489
  51.7 28.8 %collective-permute-start.7 = (bf16[240,384]{1,0:T(8,128)(2,1)S(1)}, bf16[240,384]{1,0:T(8,128)(2,1)S(1)}, u32[]{:S(2)}, u32[]{:S(2)}) collective-permute-start(bf16[240,384]{1,0:T(8,128)(2,1)S(1)} %pad_maximum_fusion.5), channel_id=1, source_target_pairs={{0,2},{1,3},{2,0},{3,1},{4,6},{5,7},{6,4},{7,5},{8,10},{9,11},{10,... | collective-permute-start | bytes 552968 | tf_op jit(solution)/shard_map/ppermute | solution.py:489
  87.3 34.9 %collective-permute-start.9 = (bf16[3,240,384]{2,1,0:T(8,128)(2,1)S(1)}, bf16[3,240,384]{2,1,0:T(8,128)(2,1)S(1)}, u32[]{:S(2)}, u32[]{:S(2)}) collective-permute-start(bf16[3,240,384]{2,1,0:T(8,128)(2,1)S(1)} %pad_maximum_fusion.1.p0), channel_id=1, source_target_pairs={{0,8},{4,12},{8,0},{12,4},{16,24},{20,28},{24,16},{28,20},{1,9},{5... | collective-permute-start | bytes 1658888 | tf_op jit(solution)/shard_map/ppermute | solution.py:493
  163.5 29.6 %collective-permute-start.38 = (bf16[3,144,384]{2,1,0:T(8,128)(2,1)S(1)}, bf16[3,144,384]{2,1,0:T(8,128)(2,1)S(1)}, u32[]{:S(2)}, u32[]{:S(2)}) collective-permute-start(bf16[3,144,384]{2,1,0:T(8,128)(2,1)S(1)} %pad_maximum_fusion.3.refs_0_), channel_id=1, source_target_pairs={{0,4},{4,0},{8,12},{12,8},{16,20},{20,16},{24,28},{28,24},{1,5},{5... | collective-permute-start | bytes 995336 | tf_op jit(solution)/shard_map/ppermute | solution.py:493
  163.8 29.3 %collective-permute-start.39 = (bf16[3,144,384]{2,1,0:T(8,128)(2,1)}, bf16[3,144,384]{2,1,0:T(8,128)(2,1)S(1)}, u32[]{:S(2)}, u32[]{:S(2)}) collective-permute-start(bf16[3,144,384]{2,1,0:T(8,128)(2,1)} %copy-done.36), channel_id=1, source_target_pairs={{0,4},{4,0},{8,12},{12,8},{16,20},{20,16},{24,28},{28,24},{1,5},{5... | collective-permute-start | bytes 995336 | tf_op jit(solution)/shard_map/ppermute | solution.py:493
  164.1 29.1 %collective-permute-start.40 = (bf16[3,144,384]{2,1,0:T(8,128)(2,1)}, bf16[3,144,384]{2,1,0:T(8,128)(2,1)S(1)}, u32[]{:S(2)}, u32[]{:S(2)}) collective-permute-start(bf16[3,144,384]{2,1,0:T(8,128)(2,1)} %copy-done.37), channel_id=1, source_target_pairs={{0,4},{4,0},{8,12},{12,8},{16,20},{20,16},{24,28},{28,24},{1,5},{5... | collective-permute-start | bytes 995336 | tf_op jit(solution)/shard_map/ppermute | solution.py:493
  164.3 28.9 %collective-permute-start.41 = (bf16[3,144,384]{2,1,0:T(8,128)(2,1)}, bf16[3,144,384]{2,1,0:T(8,128)(2,1)S(1)}, u32[]{:S(2)}, u32[]{:S(2)}) collective-permute-start(bf16[3,144,384]{2,1,0:T(8,128)(2,1)} %collective-permute-done.37.refs_3_), channel_id=1, source_target_pairs={{0,4},{4,0},{8,12},{12,8},{16,20},{20,16},{24,28},{28,24},{1,5},{5... | collective-permute-start | bytes 995336 | tf_op jit(solution)/shard_map/ppermute | solution.py:493
  192.8 50.5 %collective-permute-start.59 = (f32[10,768]{1,0:T(8,128)S(1)}, f32[10,768]{1,0:T(8,128)S(1)}, u32[]{:S(2)}, u32[]{:S(2)}) collective-permute-start(f32[10,768]{1,0:T(8,128)S(1)} %pad_maximum_fusion.7), channel_id=1, source_target_pairs={{0,4},{4,0},{8,12},{12,8},{16,20},{20,16},{24,28},{28,24},{1,5},{5... | collective-permute-start | bytes 92168 | tf_op jit(solution)/shard_map/ppermute | solution.py:493
  270.6 65.9 %collective-permute-start.26 = (bf16[512,768]{1,0:T(8,128)(2,1)}, bf16[512,768]{1,0:T(8,128)(2,1)}, u32[]{:S(2)}, u32[]{:S(2)}) collective-permute-start(bf16[512,768]{1,0:T(8,128)(2,1)} %get-tuple-element.59), channel_id=1, source_target_pairs={{0,1},{1,0},{2,3},{3,2},{4,5},{5,4},{6,7},{7,6},{8,9},{9,8},{10,11... | collective-permute-start | bytes 2359304 | tf_op jit(solution)/shard_map/ppermute | solution.py:489
  271.8 65.4 %collective-permute-start.27 = (bf16[512,768]{1,0:T(8,128)(2,1)}, bf16[512,768]{1,0:T(8,128)(2,1)}, u32[]{:S(2)}, u32[]{:S(2)}) collective-permute-start(bf16[512,768]{1,0:T(8,128)(2,1)} %get-tuple-element.59), channel_id=1, source_target_pairs={{0,2},{1,3},{2,0},{3,1},{4,6},{5,7},{6,4},{7,5},{8,10},{9,11},{10,... | collective-permute-start | bytes 2359304 | tf_op jit(solution)/shard_map/ppermute | solution.py:489
  272.7 96.9 %collective-permute-start.74 = (bf16[4,4,96,768]{3,2,1,0:T(8,128)(2,1)}, bf16[4,4,96,768]{3,2,1,0:T(8,128)(2,1)}, u32[]{:S(2)}, u32[]{:S(2)}) collective-permute-start(bf16[4,4,96,768]{3,2,1,0:T(8,128)(2,1)} %get-tuple-element.91), channel_id=1, source_target_pairs={{0,4},{4,0},{8,12},{12,8},{16,20},{20,16},{24,28},{28,24},{1,5},{5... | collective-permute-start | bytes 7077896 | tf_op jit(solution)/shard_map/ppermute | solution.py:493
  272.7 60.0 %collective-permute-start.42 = (bf16[512,768]{1,0:T(8,128)(2,1)}, bf16[512,768]{1,0:T(8,128)(2,1)}, u32[]{:S(2)}, u32[]{:S(2)}) collective-permute-start(bf16[512,768]{1,0:T(8,128)(2,1)} %convert_element_type.284), channel_id=1, source_target_pairs={{0,1},{1,0},{2,3},{3,2},{4,5},{5,4},{6,7},{7,6},{8,9},{9,8},{10,11... | collective-permute-start | bytes 2359304 | tf_op jit(solution)/shard_map/ppermute | solution.py:489
  273.3 47.5 %collective-permute-start.62 = (f32[6,768]{1,0:T(8,128)S(1)}, f32[6,768]{1,0:T(8,128)S(1)}, u32[]{:S(2)}, u32[]{:S(2)}) collective-permute-start(f32[6,768]{1,0:T(8,128)S(1)} %slice.257), channel_id=1, source_target_pairs={{0,1},{1,0},{2,3},{3,2},{4,5},{5,4},{6,7},{7,6},{8,9},{9,8},{10,11... | collective-permute-start | bytes 55304 | tf_op jit(solution)/shard_map/ppermute | solution.py:489
  332.7 86.0 %collective-permute-start.64 = (bf16[4,4,96,768]{3,2,1,0:T(8,128)(2,1)S(1)}, bf16[4,4,96,768]{3,2,1,0:T(8,128)(2,1)S(1)}, u32[]{:S(2)}, u32[]{:S(2)}) collective-permute-start(bf16[4,4,96,768]{3,2,1,0:T(8,128)(2,1)S(1)} %copy-done.27), channel_id=1, source_target_pairs={{0,4},{4,0},{8,12},{12,8},{16,20},{20,16},{24,28},{28,24},{1,5},{5... | collective-permute-start | bytes 7077896 | tf_op jit(solution)/shard_map/ppermute | solution.py:493
  336.7 84.1 %collective-permute-start.46 = (bf16[4,4,96,768]{3,2,1,0:T(8,128)(2,1)S(1)}, bf16[4,4,96,768]{3,2,1,0:T(8,128)(2,1)S(1)}, u32[]{:S(2)}, u32[]{:S(2)}) collective-permute-start(bf16[4,4,96,768]{3,2,1,0:T(8,128)(2,1)S(1)} %copy-done.28), channel_id=1, source_target_pairs={{0,4},{4,0},{8,12},{12,8},{16,20},{20,16},{24,28},{28,24},{1,5},{5... | collective-permute-start | bytes 7077896 | tf_op jit(solution)/shard_map/ppermute | solution.py:493
  337.2 29.9 %collective-permute-start.43 = (bf16[512,768]{1,0:T(8,128)(2,1)S(1)}, bf16[512,768]{1,0:T(8,128)(2,1)S(1)}, u32[]{:S(2)}, u32[]{:S(2)}) collective-permute-start(bf16[512,768]{1,0:T(8,128)(2,1)S(1)} %get-tuple-element.131), channel_id=1, source_target_pairs={{0,1},{1,0},{2,3},{3,2},{4,5},{5,4},{6,7},{7,6},{8,9},{9,8},{10,11... | collective-permute-start | bytes 2359304 | tf_op jit(solution)/shard_map/ppermute | solution.py:489
  353.7 62.6 %collective-permute-start.44 = (bf16[512,768]{1,0:T(8,128)(2,1)S(1)}, bf16[512,768]{1,0:T(8,128)(2,1)S(1)}, u32[]{:S(2)}, u32[]{:S(2)}) collective-permute-start(bf16[512,768]{1,0:T(8,128)(2,1)S(1)} %get-tuple-element.131), channel_id=1, source_target_pairs={{0,2},{1,3},{2,0},{3,1},{4,6},{5,7},{6,4},{7,5},{8,10},{9,11},{10,... | collective-permute-start | bytes 2359304 | tf_op jit(solution)/shard_map/ppermute | solution.py:489
  367.1 49.4 %collective-permute-start.45 = (bf16[512,768]{1,0:T(8,128)(2,1)S(1)}, bf16[512,768]{1,0:T(8,128)(2,1)S(1)}, u32[]{:S(2)}, u32[]{:S(2)}) collective-permute-start(bf16[512,768]{1,0:T(8,128)(2,1)S(1)} %get-tuple-element.131), channel_id=1, source_target_pairs={{0,3},{1,2},{2,1},{3,0},{4,7},{5,6},{6,5},{7,4},{8,11},{9,10},{10,... | collective-permute-start | bytes 2359304 | tf_op jit(solution)/shard_map/ppermute | solution.py:489
  371.5 50.5 %collective-permute-start.75 = (bf16[4,96,768]{2,1,0:T(8,128)(2,1)S(1)}, bf16[4,96,768]{2,1,0:T(8,128)(2,1)S(1)}, u32[]{:S(2)}, u32[]{:S(2)}) collective-permute-start(bf16[4,96,768]{2,1,0:T(8,128)(2,1)S(1)} %get-tuple-element.132), channel_id=1, source_target_pairs={{0,8},{4,12},{8,0},{12,4},{16,24},{20,28},{24,16},{28,20},{1,9},{5... | collective-permute-start | bytes 1769480 | tf_op jit(solution)/shard_map/ppermute | solution.py:493
  416.6 35.1 %collective-permute-start.76 = (bf16[4,96,768]{2,1,0:T(8,128)(2,1)S(1)}, bf16[4,96,768]{2,1,0:T(8,128)(2,1)S(1)}, u32[]{:S(2)}, u32[]{:S(2)}) collective-permute-start(bf16[4,96,768]{2,1,0:T(8,128)(2,1)S(1)} %get-tuple-element.134), channel_id=1, source_target_pairs={{0,16},{4,20},{8,24},{12,28},{16,0},{20,4},{24,8},{28,12},{1,17},{... | collective-permute-start | bytes 1769480 | tf_op jit(solution)/shard_map/ppermute | solution.py:493
  417.6 35.1 %collective-permute-start.77 = (bf16[4,96,768]{2,1,0:T(8,128)(2,1)S(1)}, bf16[4,96,768]{2,1,0:T(8,128)(2,1)S(1)}, u32[]{:S(2)}, u32[]{:S(2)}) collective-permute-start(bf16[4,96,768]{2,1,0:T(8,128)(2,1)S(1)} %get-tuple-element.133), channel_id=1, source_target_pairs={{0,24},{4,28},{8,16},{12,20},{16,8},{20,12},{24,0},{28,4},{1,25},{... | collective-permute-start | bytes 1769480 | tf_op jit(solution)/shard_map/ppermute | solution.py:493
  420.0 34.8 %collective-permute-start.65 = (bf16[4,96,768]{2,1,0:T(8,128)(2,1)S(1)}, bf16[4,96,768]{2,1,0:T(8,128)(2,1)S(1)}, u32[]{:S(2)}, u32[]{:S(2)}) collective-permute-start(bf16[4,96,768]{2,1,0:T(8,128)(2,1)S(1)} %get-tuple-element.135), channel_id=1, source_target_pairs={{0,8},{4,12},{8,0},{12,4},{16,24},{20,28},{24,16},{28,20},{1,9},{5... | collective-permute-start | bytes 1769480 | tf_op jit(solution)/shard_map/ppermute | solution.py:493
  420.8 52.0 %collective-permute-start.66 = (bf16[4,96,768]{2,1,0:T(8,128)(2,1)S(1)}, bf16[4,96,768]{2,1,0:T(8,128)(2,1)S(1)}, u32[]{:S(2)}, u32[]{:S(2)}) collective-permute-start(bf16[4,96,768]{2,1,0:T(8,128)(2,1)S(1)} %get-tuple-element.137), channel_id=1, source_target_pairs={{0,16},{4,20},{8,24},{12,28},{16,0},{20,4},{24,8},{28,12},{1,17},{... | collective-permute-start | bytes 1769480 | tf_op jit(solution)/shard_map/ppermute | solution.py:493
  422.0 66.5 %collective-permute-start.67 = (bf16[4,96,768]{2,1,0:T(8,128)(2,1)S(1)}, bf16[4,96,768]{2,1,0:T(8,128)(2,1)S(1)}, u32[]{:S(2)}, u32[]{:S(2)}) collective-permute-start(bf16[4,96,768]{2,1,0:T(8,128)(2,1)S(1)} %get-tuple-element.136), channel_id=1, source_target_pairs={{0,24},{4,28},{8,16},{12,20},{16,8},{20,12},{24,0},{28,4},{1,25},{... | collective-permute-start | bytes 1769480 | tf_op jit(solution)/shard_map/ppermute | solution.py:493
  451.7 37.4 %collective-permute-start.47 = (bf16[4,96,768]{2,1,0:T(8,128)(2,1)S(1)}, bf16[4,96,768]{2,1,0:T(8,128)(2,1)S(1)}, u32[]{:S(2)}, u32[]{:S(2)}) collective-permute-start(bf16[4,96,768]{2,1,0:T(8,128)(2,1)S(1)} %get-tuple-element.138), channel_id=1, source_target_pairs={{0,8},{4,12},{8,0},{12,4},{16,24},{20,28},{24,16},{28,20},{1,9},{5... | collective-permute-start | bytes 1769480 | tf_op jit(solution)/shard_map/ppermute | solution.py:493
  452.7 39.4 %collective-permute-start.48 = (bf16[4,96,768]{2,1,0:T(8,128)(2,1)S(1)}, bf16[4,96,768]{2,1,0:T(8,128)(2,1)S(1)}, u32[]{:S(2)}, u32[]{:S(2)}) collective-permute-start(bf16[4,96,768]{2,1,0:T(8,128)(2,1)S(1)} %get-tuple-element.140), channel_id=1, source_target_pairs={{0,16},{4,20},{8,24},{12,28},{16,0},{20,4},{24,8},{28,12},{1,17},{... | collective-permute-start | bytes 1769480 | tf_op jit(solution)/shard_map/ppermute | solution.py:493
  454.8 54.6 %collective-permute-start.49 = (bf16[4,96,768]{2,1,0:T(8,128)(2,1)S(1)}, bf16[4,96,768]{2,1,0:T(8,128)(2,1)S(1)}, u32[]{:S(2)}, u32[]{:S(2)}) collective-permute-start(bf16[4,96,768]{2,1,0:T(8,128)(2,1)S(1)} %get-tuple-element.139), channel_id=1, source_target_pairs={{0,24},{4,28},{8,16},{12,20},{16,8},{20,12},{24,0},{28,4},{1,25},{... | collective-permute-start | bytes 1769480 | tf_op jit(solution)/shard_map/ppermute | solution.py:493
  472.8 37.0 %collective-permute-start.78 = (bf16[96,768]{1,0:T(8,128)(2,1)S(1)}, bf16[96,768]{1,0:T(8,128)(2,1)S(1)}, u32[]{:S(2)}, u32[]{:S(2)}) collective-permute-start(bf16[96,768]{1,0:T(8,128)(2,1)S(1)} %get-tuple-element.141), channel_id=1, source_target_pairs={{0,1},{1,0},{2,3},{3,2},{4,5},{5,4},{6,7},{7,6},{8,9},{9,8},{10,11... | collective-permute-start | bytes 442376 | tf_op jit(solution)/shard_map/ppermute | solution.py:489
  492.1 40.9 %collective-permute-start.68 = (bf16[96,768]{1,0:T(8,128)(2,1)S(1)}, bf16[96,768]{1,0:T(8,128)(2,1)S(1)}, u32[]{:S(2)}, u32[]{:S(2)}) collective-permute-start(bf16[96,768]{1,0:T(8,128)(2,1)S(1)} %get-tuple-element.144), channel_id=1, source_target_pairs={{0,1},{1,0},{2,3},{3,2},{4,5},{5,4},{6,7},{7,6},{8,9},{9,8},{10,11... | collective-permute-start | bytes 442376 | tf_op jit(solution)/shard_map/ppermute | solution.py:489
  (95 other events, 2431.3 us)
